TPU v7x, 256 devices: a whole 4x4x8 slice. The times are simulated.
256 devices in a mesh: seq: 32 (over z, y), grp: 8 (over x, core).
Axes of the slice: x: 4, y: 4, z: 8, core: 2. Of those that a mesh axis runs over, the one named last changes fastest.
Arguments:
- output_grad: bfloat16 [32768, 4096], P(('seq', 'grp')), may hold values from -24 to 24
- router_logit: float32 [32768], P(('seq', 'grp')), may hold values from -6 to 6
- chosen_index: int32 [8192], P(('seq', 'grp')), may hold values from 0 to 127, as said below
- chosen_count: int32 [256], replicated, may hold values from 0 to 32, as said below
- out_weight: bfloat16 [2048, 4096], P('grp'), may hold values from -0.125 to 0.125
- queries: bfloat16 [4096, 2048], P('seq', 'grp'), may hold values from -6 to 6
- key_rows: bfloat16 [4096, 2048], P('seq', 'grp'), may hold values from -6 to 6
- value_rows: bfloat16 [4096, 2048], P('seq', 'grp'), may hold values from -6 to 6
Outputs:
- query_grad: bfloat16 [4096, 2048], P('seq', 'grp')
- key_grad: bfloat16 [4096, 2048], P('seq', 'grp')
- value_grad: bfloat16 [4096, 2048], P('seq', 'grp')
- out_weight_grad: float32 [4096, 2048], P('seq', 'grp')
- logit_grad: float32 [32768], P(('seq', 'grp'))
Inputs may be any that keep to these rules, and one draw needn't show every extreme that they name: `chosen_count`: for each seq index, the counts of its 8 shards (consecutive in the list) sum to 128. `chosen_index`: in each shard's 32 slots the first chosen_count entries are distinct local token positions in increasing order; the other slots hold 0.
All inputs are finite; a program needn't handle non-finite values.
Results may differ from a plain program's by a relative error of at most 0.034.
Values may be sent and summed in bfloat16 or wider, within the bound.
A program may use at most 64 MiB of HBM per device.

v0:
```python
import jax
import jax.numpy as jnp
from jax import lax
from jax.sharding import PartitionSpec as P

HD = 128


def split_heads(rows):
    return rows.reshape(rows.shape[0], rows.shape[1] // HD, HD)


def block_scores(query_heads, key_block, query_pos, key_first, factor):
    scores = (
        jnp.einsum("qhd,khd->hqk", query_heads, key_block, preferred_element_type=jnp.float32)
        * factor
    )
    key_pos = key_first + jnp.arange(key_block.shape[0])
    allowed = query_pos[:, None] >= key_pos[None, :]
    return (scores, allowed)


def back_terms(
    query_heads,
    grad_heads,
    log_norm,
    row_delta,
    key_block,
    value_block,
    query_pos,
    key_first,
    factor,
):
    scores, allowed = block_scores(query_heads, key_block, query_pos, key_first, factor)
    weights = jnp.exp(jnp.where(allowed[None], scores - log_norm[:, :, None], -jnp.inf))
    weights_bf = weights.astype(jnp.bfloat16)
    grad_weights = jnp.einsum(
        "qhd,khd->hqk", grad_heads, value_block, preferred_element_type=jnp.float32
    )
    grad_scores = (weights * (grad_weights - row_delta[:, :, None])).astype(jnp.bfloat16)
    return (weights_bf, grad_scores)


def shards(
    output_grad, router_logit, chosen_index, chosen_count, out_weight, queries, key_rows, value_rows
):
    factor = HD ** (-0.5)
    groups = lax.axis_size("grp")
    seq_here = lax.axis_index("seq")
    shard_here = seq_here * groups + lax.axis_index("grp")
    capacity = chosen_index.shape[0]
    block_len = queries.shape[0]
    local_cols = queries.shape[1]
    local_heads = local_cols // HD
    slot_ids = jnp.arange(capacity)
    own_count = lax.dynamic_slice_in_dim(chosen_count, shard_here, 1)[0]
    live_slots = slot_ids < own_count
    picked = jnp.where(
        live_slots[:, None], output_grad[chosen_index], jnp.zeros((), output_grad.dtype)
    )
    sigmoid_val = jax.nn.sigmoid(router_logit[chosen_index])
    gate_bf = sigmoid_val.astype(jnp.bfloat16)
    all_rows, all_gates = (
        lax.all_gather(picked, "grp", axis=0, tiled=True),
        lax.all_gather(gate_bf, "grp", axis=0, tiled=True),
    )
    group_counts = lax.dynamic_slice_in_dim(chosen_count, seq_here * groups, groups)
    group_ends = jnp.cumsum(group_counts)
    starts = group_ends - group_counts
    block_pos = jnp.arange(block_len)
    owner_ids = jnp.sum((block_pos[:, None] >= group_ends[None, :]).astype(jnp.int32), axis=1)
    onehot = owner_ids[:, None] == jnp.arange(groups)[None, :]
    offset = jnp.sum(jnp.where(onehot, starts[None, :], 0), axis=1)
    source = owner_ids * capacity + block_pos - offset
    grad_block = all_rows[source]
    gate_block = all_gates[source].astype(jnp.float32)
    query_heads = split_heads(queries)
    keys_all, values_all = (
        lax.all_gather(key_rows, "seq", axis=0, tiled=True),
        lax.all_gather(value_rows, "seq", axis=0, tiled=True),
    )
    key_width = 4 * block_len
    first_row = seq_here * block_len
    needed = (first_row + block_len - 1) // key_width + 1
    query_pos = first_row + block_pos

    def key_slice(block_index):
        key_block = split_heads(
            lax.dynamic_slice_in_dim(keys_all, block_index * key_width, key_width)
        )
        value_block = split_heads(
            lax.dynamic_slice_in_dim(values_all, block_index * key_width, key_width)
        )
        return (key_block, value_block)

    def stats_step(block_index, totals):
        row_max, row_sum = totals
        key_block, value_block = key_slice(block_index)
        scores, allowed = block_scores(
            query_heads, key_block, query_pos, block_index * key_width, factor
        )
        masked = jnp.where(allowed[None], scores, -jnp.inf)
        new_max = jnp.maximum(row_max, jnp.max(masked, axis=2))
        row_sum = row_sum * jnp.exp(row_max - new_max) + jnp.sum(
            jnp.exp(masked - new_max[:, :, None]), axis=2
        )
        return (new_max, row_sum)

    init_max = jnp.full((local_heads, block_len), -1e30, jnp.float32)
    init_sum = jnp.zeros((local_heads, block_len), jnp.float32)
    row_max, row_sum = lax.fori_loop(0, needed, stats_step, (init_max, init_sum))
    log_norm = row_max + jnp.log(row_sum)

    def output_step(block_index, running):
        key_block, value_block = key_slice(block_index)
        scores, allowed = block_scores(
            query_heads, key_block, query_pos, block_index * key_width, factor
        )
        weights = jnp.exp(jnp.where(allowed[None], scores - log_norm[:, :, None], -jnp.inf)).astype(
            jnp.bfloat16
        )
        return running + jnp.einsum(
            "hqk,khd->qhd", weights, value_block, preferred_element_type=jnp.float32
        )

    out_acc = lax.fori_loop(
        0, needed, output_step, jnp.zeros((block_len, local_heads, HD), jnp.float32)
    )
    attn_out = out_acc.reshape(block_len, local_cols).astype(jnp.bfloat16)
    projected = lax.dot_general(
        grad_block, out_weight, (((1,), (1,)), ((), ())), preferred_element_type=jnp.float32
    )
    router_part = jnp.sum(attn_out.astype(jnp.float32) * projected, axis=1)
    out_grad_bf = (gate_block[:, None] * projected).astype(jnp.bfloat16)
    gated_out = (gate_block[:, None] * attn_out.astype(jnp.float32)).astype(jnp.bfloat16)
    out_weight_grad = lax.psum_scatter(
        lax.dot_general(
            grad_block, gated_out, (((0,), (0,)), ((), ())), preferred_element_type=jnp.float32
        ).astype(jnp.bfloat16),
        "seq",
        scatter_dimension=0,
        tiled=True,
    ).astype(jnp.float32)
    padded = jnp.zeros((groups * capacity,), jnp.float32).at[source].set(router_part)
    own_part = lax.psum_scatter(padded, "grp", scatter_dimension=0, tiled=True)
    logit_term = jnp.where(live_slots, own_part * sigmoid_val * (1.0 - sigmoid_val), 0.0)
    logit_grad = jnp.zeros(router_logit.shape, jnp.float32).at[chosen_index].add(logit_term)
    grad_heads = split_heads(out_grad_bf)
    out_heads = split_heads(attn_out)
    row_delta = jnp.sum(grad_heads.astype(jnp.float32) * out_heads.astype(jnp.float32), axis=2).T
    query_zero = jnp.zeros((block_len, local_heads, HD), jnp.float32)

    def back_step(block_index, totals):
        query_acc, key_acc, value_acc = totals
        key_block, value_block = key_slice(block_index)
        row_start = block_index * key_width
        weights_bf, grad_scores = back_terms(
            query_heads,
            grad_heads,
            log_norm,
            row_delta,
            key_block,
            value_block,
            query_pos,
            row_start,
            factor,
        )
        query_acc = query_acc + jnp.einsum(
            "hqk,khd->qhd", grad_scores, key_block, preferred_element_type=jnp.float32
        )
        key_part = jnp.einsum(
            "hqk,qhd->khd", grad_scores, query_heads, preferred_element_type=jnp.float32
        )
        value_part = jnp.einsum(
            "hqk,qhd->khd", weights_bf, grad_heads, preferred_element_type=jnp.float32
        )
        key_acc = lax.dynamic_update_slice_in_dim(
            key_acc,
            lax.dynamic_slice_in_dim(key_acc, row_start, key_width) + key_part,
            row_start,
            0,
        )
        value_acc = lax.dynamic_update_slice_in_dim(
            value_acc,
            lax.dynamic_slice_in_dim(value_acc, row_start, key_width) + value_part,
            row_start,
            0,
        )
        return (query_acc, key_acc, value_acc)

    all_zero = jnp.zeros((keys_all.shape[0], local_heads, HD), jnp.float32)
    query_acc, key_acc, value_acc = lax.fori_loop(
        0, needed, back_step, (query_zero, all_zero, all_zero)
    )
    key_sum, value_sum = (
        lax.psum_scatter(
            key_acc.reshape(-1, local_cols).astype(jnp.bfloat16),
            "seq",
            scatter_dimension=0,
            tiled=True,
        ).astype(jnp.float32),
        lax.psum_scatter(
            value_acc.reshape(-1, local_cols).astype(jnp.bfloat16),
            "seq",
            scatter_dimension=0,
            tiled=True,
        ).astype(jnp.float32),
    )
    key_grad = (key_sum * factor).astype(jnp.bfloat16)
    value_grad = value_sum.astype(jnp.bfloat16)
    query_grad = (query_acc * factor).reshape(block_len, local_cols).astype(jnp.bfloat16)
    return (query_grad, key_grad, value_grad, out_weight_grad, logit_grad)


def solution(mesh):
    placed = (
        P(("seq", "grp"), None),
        P(("seq", "grp")),
        P(("seq", "grp")),
        P(),
        P("grp", None),
        P("seq", "grp"),
        P("seq", "grp"),
        P("seq", "grp"),
    )
    return jax.shard_map(
        shards,
        mesh=mesh,
        in_specs=placed,
        out_specs=(
            P("seq", "grp"),
            P("seq", "grp"),
            P("seq", "grp"),
            P("seq", "grp"),
            P(("seq", "grp")),
        ),
        check_vma=False,
    )
```

profile of v0, /device:TPU:1, one launch (start us, length us, event | category | flops | bytes accessed | tf_op | source)
XLA Modules:
  0.0 919.4 jit_solution(15352564952240310597)
XLA Ops:
  10.0 2.3 gather_fusion.2
  18.9 26.3 %all-gather.8.cloned.1.call-done = bf16[256,4096]{1,0:T(8,128)(2,1)} async-done(((bf16[32,4096]{1,0:T(8,128)(2,1)}), bf16[256,4096]{1,0:T(8,128)(2,1)}) %all-gather.8.cloned.1.call-update) | async-done | bytes 2097168 | tf_op jit(solution)/shard_map/all_gather | solution.py:64
  45.2 4.1 gather_fusion.3
  49.3 70.6 %all-gather.4.cloned.1.call-done = bf16[4096,256]{0,1:T(8,128)(2,1)} async-done(((bf16[128,256]{0,1:T(8,128)(2,1)}), bf16[4096,256]{0,1:T(8,128)(2,1)}) %all-gather.4.cloned.1.call-update) | async-done | bytes 2097168 | tf_op jit(solution)/shard_map/all_gather | solution.py:79
  119.9 1.6 while.39
  121.5 75.5 %all-gather.6.cloned.1.call-done = bf16[4096,256]{0,1:T(8,128)(2,1)} async-done(((bf16[128,256]{0,1:T(8,128)(2,1)}), bf16[4096,256]{0,1:T(8,128)(2,1)}) %all-gather.6.cloned.1.call-update) | async-done | bytes 2097168 | tf_op jit(solution)/shard_map/all_gather | solution.py:80
  197.7 4.0 while.40
  197.9 1.8 constant_dynamic-slice_fusion.9
  199.6 2.1 fusion.92
  204.8 15.4 %all-reduce.1 = f32[256]{0:T(256)S(1)} all-reduce(f32[256]{0:T(256)S(1)} %scatter_custom_fusion), channel_id=5, replica_groups=mesh['seq'=32,'grp'=8] {'grp'}, use_global_device_ids=true, to_apply=%region_17.18.clone | all-reduce | flops 256 | bytes 2048
  221.6 12.4 %all-reduce = bf16[256]{0:T(256)(128)(2,1)S(1)} all-reduce(bf16[256]{0:T(256)(128)(2,1)S(1)} %dynamic-update-slice), channel_id=1, replica_groups=mesh['seq'=32,'grp'=8] {'grp'}, use_global_device_ids=true, to_apply=%add | all-reduce | flops 256 | bytes 1024
  236.1 2.1 convolution_convert_fusion
  239.3 2.2 broadcast_in_dim.100.clone
  241.6 2.2 broadcast_in_dim.100
  243.8 6.2 while.41
  245.8 2.1 fusion.107
  247.9 2.1 fusion.106
  250.0 3.8 copy_bitcast_fusion.1
  253.8 3.7 copy_bitcast_fusion
  259.7 215.3 %reduce-scatter.8.cloned.1.call-done = bf16[128,256]{1,0:T(8,128)(2,1)} async-done(((bf16[4096,256]{1,0:T(8,128)(2,1)}), bf16[128,256]{1,0:T(8,128)(2,1)}) %reduce-scatter.8.cloned.1.call-update) | async-done | bytes 65552 | tf_op jit(solution)/shard_map/reduce_scatter | solution.py:136
  475.0 1.5 convert_element_type.97
  476.5 216.9 %reduce-scatter.4.cloned.1.call-done = bf16[128,256]{1,0:T(8,128)(2,1)} async-done(((bf16[4096,256]{1,0:T(8,128)(2,1)}), bf16[128,256]{1,0:T(8,128)(2,1)}) %reduce-scatter.4.cloned.1.call-update) | async-done | bytes 65552 | tf_op jit(solution)/shard_map/reduce_scatter | solution.py:196
  693.4 1.5 multiply_convert_fusion.1
  694.9 217.6 %reduce-scatter.6.cloned.1.call-done = bf16[128,256]{1,0:T(8,128)(2,1)} async-done(((bf16[4096,256]{1,0:T(8,128)(2,1)}), bf16[128,256]{1,0:T(8,128)(2,1)}) %reduce-scatter.6.cloned.1.call-update) | async-done | bytes 65552 | tf_op jit(solution)/shard_map/reduce_scatter | solution.py:202
  (88 shorter events, 22.1 us)
Async XLA Ops:
  7.2 195.6 %copy-start = (bf16[256,4096]{1,0:T(8,128)(2,1)S(1)}, bf16[256,4096]{1,0:T(8,128)(2,1)}, u32[]{:S(2)}) copy-start(bf16[256,4096]{1,0:T(8,128)(2,1)} %param.18) | copy-start | bytes 6291460
  7.2 7.7 copy-start.8
  7.2 6.0 copy-start.3
  7.2 6.8 copy-start.4
  7.2 8.8 copy-start.1
  7.2 9.5 %copy-start.5 = (bf16[128,256]{1,0:T(8,128)(2,1)S(1)}, bf16[128,256]{1,0:T(8,128)(2,1)}, u32[]{:S(2)}) copy-start(bf16[128,256]{1,0:T(8,128)(2,1)} %param.19) | copy-start | bytes 196612
  7.2 38.0 %all-gather.8.cloned.1.call-start = ((), (), s32[]{:S(2)}) async-start(), calls=%async_computation.5 | async-start | bytes 2359296 | tf_op jit(solution)/shard_map/all_gather | solution.py:64
  10.0 7.0 copy-start.6
  13.2 106.7 %all-gather.4.cloned.1.call-start = ((), (), s32[]{:S(2)}) async-start(), calls=%async_computation.3 | async-start | bytes 2162688 | tf_op jit(solution)/shard_map/all_gather | solution.py:79
  14.0 183.1 %all-gather.6.cloned.1.call-start = ((), (), s32[]{:S(2)}) async-start(), calls=%async_computation.4 | async-start | bytes 2162688 | tf_op jit(solution)/shard_map/all_gather | solution.py:80
  14.8 460.2 %reduce-scatter.8.cloned.1.call-start = ((), (), s32[]{:S(2)}) async-start(), calls=%async_computation.8 | async-start | bytes 2162688 | tf_op jit(solution)/shard_map/reduce_scatter | solution.py:136
  15.4 0.6 copy-start.7
  236.1 3.1 copy-start.2
  239.3 454.2 %reduce-scatter.4.cloned.1.call-start = ((), (), s32[]{:S(2)}) async-start(), calls=%async_computation.6 | async-start | bytes 2162688 | tf_op jit(solution)/shard_map/reduce_scatter | solution.py:196
  253.8 658.8 %reduce-scatter.6.cloned.1.call-start = ((), (), s32[]{:S(2)}) async-start(), calls=%async_computation.7 | async-start | bytes 2162688 | tf_op jit(solution)/shard_map/reduce_scatter | solution.py:202
Sparse Core Ops, SparseCore 0:
  13.3 31.8 all-gather.7
  48.3 71.6 all-gather.3
  123.0 74.0 all-gather.5
  239.4 235.5 reduce-scatter.7
  479.1 214.2 reduce-scatter.3
  697.7 214.7 reduce-scatter.5
where the time goes:
time: 926 us; the launch traced here: 919 us
  waiting for transfers between devices  822 us (89%)
  blocking collectives  27.8 us (3%)
  local copies, waits for them, and re-layouts  24.7 us (3%)
  other arithmetic  18 us (2%)
  between operations  15.7 us (2%)
  matrix products  10.4 us (1%)
    reduce_scatter x1, waiting for transfers between devices, shards(): lax.psum_scatter(value_acc.reshape(-1, local_cols).astype(jnp.bfloat16),...  218 us
    reduce_scatter x1, waiting for transfers between devices, shards(): lax.psum_scatter(key_acc.reshape(-1, local_cols).astype(jnp.bfloat16), 's...  217 us
    reduce_scatter x1, waiting for transfers between devices, shards(): lax.psum_scatter(lax.dot_general(grad_block, gated_out, (((0,), (0,)), ((...  215 us
    all_gather x1, waiting for transfers between devices, shards(): lax.all_gather(value_rows, 'seq', axis=0, tiled=True)  75.5 us
    all_gather x1, waiting for transfers between devices, shards(): lax.all_gather(key_rows, 'seq', axis=0, tiled=True)  70.6 us
    unnamed x2, blocking collectives  27.8 us
    all_gather x1, waiting for transfers between devices, shards(): lax.all_gather(picked, 'grp', axis=0, tiled=True)  26.3 us
  transfers between devices with their start and end apart: 6, of which 6 were waited for; matrix products, arithmetic and copies ran while one was open for 4% of the time, Pallas kernels for 0%

commit v1 on v0

v1 whole, which is shorter than its diff:
```python
import jax
import jax.numpy as jnp
from jax import lax
from jax.experimental import pallas as pl
from jax.experimental.pallas import tpu as pltpu
from jax.sharding import PartitionSpec as P

HD = 128
NY = 4
MESH = pl.DeviceIdType.MESH
BF = jnp.bfloat16
F32 = jnp.float32
NEG = -1e30


def dot(a, b, ca, cb, precision=None):
    return lax.dot_general(
        a, b, (((ca,), (cb,)), ((), ())), preferred_element_type=F32, precision=precision
    )


class Layout:
    def __init__(self, nz, nx, tok, cap, d):
        self.nz, self.nx, self.tok, self.cap, self.d = nz, nx, tok, cap, d
        self.dh = d // 2
        self.hz = nz // 2
        self.far = nz // 2
        self.near = nz - 1 - self.far

    def scratch(self):
        nz, nx, cap, d, dh, hz = self.nz, self.nx, self.cap, self.d, self.dh, self.hz
        v = pltpu.VMEM
        steps = max(self.far, 1)
        names = dict(
            grads=v((self.tok, d), BF),
            weight=v((2, 2 * HD, dh), BF),
            picked=v((2, cap, dh + HD), BF),
            rows=v((2 * nx * cap, dh + HD), BF),
            block=v((HD, dh + HD), BF),
            slice_out=v((NY, HD, (hz + 1) * HD), BF),
            slices=v((NY * HD, (hz + 1) * HD), BF),
            proj_part=v((2, HD, 2 * HD), F32),
            proj_in=v((HD, 2 * HD), F32),
            proj=v((HD, 2 * HD), F32),
            go_out=v((2, HD, HD), BF),
            qh=v((NY, HD, HD), BF),
            goh=v((NY, HD, HD), BF),
            kk=v((nz, 2 * HD, HD), BF),
            vv=v((nz, 2 * HD, HD), BF),
            soft=v((NY, HD + 16, HD), F32),
            soft_in=v((NY, HD + 16, HD), F32),
            lse=v((NY, 8, HD), F32),
            delta=v((NY, 8, HD), F32),
            outs=v((NY, NY * HD, HD), BF),
            gated=v((NY * HD, NY * HD), BF),
            dqt=v((NY, HD, HD), F32),
            dkp=v((nz, 2 * HD, HD), F32),
            dvp=v((nz, 2 * HD, HD), F32),
            dwp=v((2, hz, HD, 2 * HD), F32),
            kv_send=v((2, 2, steps, 2 * HD, HD), BF),
            kv_recv=v((2, 2, steps, 2 * HD, HD), BF),
            dw_send=v((2, 2, steps, HD, 2 * HD), BF),
            dw_recv=v((2, 2, steps, HD, 2 * HD), BF),
            kv_fin=v((2, 2, HD, HD), BF),
            kv_land=v((2, 2, HD, HD), BF),
            dq_out=v((NY, HD, HD), BF),
            dq_land=v((2, 2, HD, HD), BF),
            dw_fin=v((2, HD, 2 * HD), F32),
            dw_land=v((HD, 2 * HD), F32),
            router=v((8, HD), F32),
            router_in=v((2 * nx, 8, HD), F32),
        )
        return names


def fused(lay, names, *refs):
    (g_ref, logit_ref, idx_ref, cnt_ref, w_ref, q_ref, k_ref, v_ref) = refs[:8]
    (dq_ref, dk_ref, dv_ref, dw_ref, lg_ref) = refs[8:13]
    buf = dict(zip(names, refs[13 : 13 + len(names)]))
    send_sems, recv_sems, local_sems = refs[13 + len(names) :]
    nz, nx, cap, dh, hz = lay.nz, lay.nx, lay.cap, lay.dh, lay.hz
    shards = 2 * nx
    factor = HD ** (-0.5)

    s, g = lax.axis_index("seq"), lax.axis_index("grp")
    z, y, x, c = s // NY, s % NY, g // 2, g % 2
    sib = 1 - c

    def dev(z_, y_, x_, c_):
        return (z_ * NY + y_, x_ * 2 + c_)

    up, down = (z + 1) % nz, (z + nz - 1) % nz
    dev_up, dev_down = dev(up, y, x, c), dev(down, y, x, c)
    dev_sib = dev(z, y, x, sib)

    counter = {"send": 0, "recv": 0, "local": 0}

    def alloc(kind, n=1):
        first = counter[kind]
        counter[kind] += n
        return first

    sent = []

    def send(src, dst, recv_id, to, unless=None):
        copy = pltpu.make_async_remote_copy(
            src_ref=src,
            dst_ref=dst,
            send_sem=send_sems.at[alloc("send")],
            recv_sem=recv_sems.at[recv_id],
            device_id=to,
            device_id_type=MESH,
        )
        sent.append((unless, copy))
        if unless is None:
            copy.start()
        else:
            pl.when(jnp.logical_not(unless))(lambda: copy.start())

    def recv(dst, recv_id, unless=None):
        copy = pltpu.make_async_remote_copy(
            src_ref=dst,
            dst_ref=dst,
            send_sem=send_sems.at[0],
            recv_sem=recv_sems.at[recv_id],
            device_id=dev_sib,
            device_id_type=MESH,
        )
        if unless is None:
            copy.wait_recv()
        else:
            pl.when(jnp.logical_not(unless))(lambda: copy.wait_recv())

    grads_in = pltpu.make_async_copy(g_ref, buf["grads"], local_sems.at[alloc("local")])
    grads_in.start()
    own_half = pl.multiple_of(c * dh, HD)
    other_half = pl.multiple_of(sib * dh, HD)
    weight_in = pltpu.make_async_copy(
        w_ref.at[:, pl.ds(own_half, dh)], buf["weight"].at[c], local_sems.at[alloc("local")]
    )
    weight_in.start()

    partners = [dev_sib, dev_up, dev_down]
    for dy in range(1, NY):
        for cc in range(2):
            partners.append(dev(z, (y + dy) % NY, x, cc))
    for dx in range(1, nx):
        for cc in range(2):
            partners.append(dev(z, y, (x + dx) % nx, cc))
    barrier = pltpu.get_barrier_semaphore()
    for partner in partners:
        pl.semaphore_signal(barrier, inc=1, device_id=partner, device_id_type=MESH)
    pl.semaphore_wait(barrier, len(partners))

    half_y = y // 2
    id_k, id_v, id_q = alloc("recv", 2), alloc("recv", 2), alloc("recv", NY)
    own_copies = []
    for j in range(2):
        y_to = 2 * c + j
        own = jnp.logical_and(y_to == y, half_y == c)
        cols = slice(j * HD, (j + 1) * HD)
        part = pl.ds(pl.multiple_of((y % 2) * HD, HD), HD)
        for src, name, base in ((k_ref, "kk", id_k), (v_ref, "vv", id_v)):
            dst = buf[name].at[z, part, :]
            send(src.at[:, cols], dst, base + y % 2, dev(z, y_to, x, half_y), own)
            own_copies.append(
                (own, pltpu.make_async_copy(src.at[:, cols], dst, local_sems.at[alloc("local")]))
            )
            pl.when(own)(lambda: own_copies[-1][1].start())
    for j in range(2):
        y_to = 2 * c + j
        cols = slice(j * HD, (j + 1) * HD)
        for cc in range(2):
            own = jnp.logical_and(y_to == y, c == cc)
            dst = buf["qh"].at[y]
            send(q_ref.at[:, cols], dst, id_q + y, dev(z, y_to, x, cc), own)
            own_copies.append(
                (own, pltpu.make_async_copy(q_ref.at[:, cols], dst, local_sems.at[alloc("local")]))
            )
            pl.when(own)(lambda: own_copies[-1][1].start())
    id_w = alloc("recv")
    send(w_ref.at[:, pl.ds(other_half, dh)], buf["weight"].at[c], id_w, dev_sib)

    slot = lax.broadcasted_iota(jnp.int32, (cap, HD), 0)
    lane = lax.broadcasted_iota(jnp.int32, (cap, HD), 1)
    index = jnp.zeros((cap, HD), jnp.int32)
    for j in range(cap):
        index = jnp.where(slot == j, idx_ref[j], index)
    first = s * shards
    starts, total = [], jnp.int32(0)
    counts = []
    for i in range(shards):
        starts.append(total)
        counts.append(cnt_ref[first + i])
        total = total + counts[-1]
    own_start, own_count = jnp.int32(0), jnp.int32(0)
    for i in range(shards):
        own_start = jnp.where(g == i, starts[i], own_start)
        own_count = jnp.where(g == i, counts[i], own_count)
    pick = jnp.logical_and(index == lane, slot < own_count)
    pick_bf = pick.astype(F32).astype(BF)
    logit_row = logit_ref[...]
    chosen_logit = jnp.sum(
        jnp.where(pick, jnp.broadcast_to(logit_row, (cap, HD)), 0.0), axis=1, keepdims=True
    )
    gate_col = 1.0 / (1.0 + jnp.exp(-chosen_logit))
    gate_tile = jnp.broadcast_to(gate_col, (cap, HD)).astype(BF)
    grads_in.wait()
    for h in range(2):
        buf["picked"][h, :, pl.ds(dh, HD)] = gate_tile
    for h in range(2):
        buf["picked"][h, :, pl.ds(0, dh)] = dot(
            pick_bf, buf["grads"][:, h * dh : (h + 1) * dh], 1, 0
        ).astype(BF)

    right, left = (x + 1) % nx, (x + nx - 1) % nx
    rows = buf["rows"]

    def row_slot(shard):
        return rows.at[pl.ds(pl.multiple_of(shard * cap, cap), cap), :]

    id_rows_sib = alloc("recv")
    id_from_left, id_from_right = alloc("recv", 2), alloc("recv", 2)
    id_far_left, id_far_right = alloc("recv"), alloc("recv")
    send(buf["picked"].at[sib], row_slot(g), id_rows_sib, dev_sib)
    if nx > 1:
        for h in range(2):
            send(buf["picked"].at[h], row_slot(g), id_from_left + c, dev(z, y, right, h))
            send(buf["picked"].at[h], row_slot(g), id_from_right + c, dev(z, y, left, h))
    rows[pl.ds(pl.multiple_of(g * cap, cap), cap), :] = buf["picked"][c]

    buf["dkp"][...] = jnp.zeros_like(buf["dkp"])
    buf["dvp"][...] = jnp.zeros_like(buf["dvp"])
    buf["dqt"][...] = jnp.zeros_like(buf["dqt"])
    soft = buf["soft"]
    soft[...] = jnp.zeros_like(soft)
    for i in range(NY):
        soft[i, HD : HD + 8, :] = jnp.full((8, HD), NEG, F32)

    kv_own = pl.ds(pl.multiple_of(0, HD), HD)
    for j in range(2):
        own = jnp.logical_and(c == half_y, y == 2 * c + j)
        part = slice(j * HD, (j + 1) * HD)
        recv(buf["kk"].at[z, part, :], id_k + j, own)
        recv(buf["vv"].at[z, part, :], id_v + j, own)
    for own, copy in own_copies:
        pl.when(own)(lambda: copy.wait())

    ring = (("kk", lay.far, lay.near), ("vv", lay.near, lay.far))
    id_up = {n: alloc("recv", lay.far + 1) for n in ("kk", "vv")}
    id_down = {n: alloc("recv", lay.far + 1) for n in ("kk", "vv")}

    def ring_send(t):
        for name, n_up, n_down in ring:
            if t <= n_up:
                b = (z + nz - t + 1) % nz
                send(buf[name].at[b], buf[name].at[b], id_up[name] + t, dev_up)
            if t <= n_down:
                b = (z + t - 1) % nz
                send(buf[name].at[b], buf[name].at[b], id_down[name] + t, dev_down)

    def ring_recv(t):
        for name, n_up, n_down in ring:
            if t <= n_up:
                recv(buf[name].at[(z + nz - t) % nz], id_up[name] + t)
            if t <= n_down:
                recv(buf[name].at[(z + t) % nz], id_down[name] + t)

    ring_send(1)

    def allowed(i):
        key = c * 2 * HD + lax.broadcasted_iota(jnp.int32, (2 * HD, HD), 0)
        query = i * HD + lax.broadcasted_iota(jnp.int32, (2 * HD, HD), 1)
        return key <= query

    def forward_block(b, diagonal):
        keys, values = buf["kk"][b], buf["vv"][b]
        for i in range(NY):
            scores = dot(keys, buf["qh"][i], 1, 1) * factor
            if diagonal:
                scores = jnp.where(allowed(i), scores, NEG)
            old = soft[i, HD : HD + 1, :]
            new = jnp.maximum(old, jnp.max(scores, axis=0, keepdims=True))
            weights = jnp.exp(scores - new)
            decay = jnp.exp(old - new)
            norm = soft[i, HD + 8 : HD + 9, :] * decay + jnp.sum(weights, axis=0, keepdims=True)
            soft[i, 0:HD, :] = soft[i, 0:HD, :] * decay + dot(values, weights.astype(BF), 0, 0)
            soft[i, HD : HD + 1, :] = new
            soft[i, HD + 8 : HD + 9, :] = norm

    def forward_pair(t):
        pl.when(z >= t)(lambda: forward_block((z + nz - t) % nz, False))
        if t <= nz - 1 - t:
            pl.when(z + t >= nz)(lambda: forward_block((z + t) % nz, False))

    for i in range(NY):
        own = jnp.logical_and(c == half_y, y == i)
        recv(buf["qh"].at[i], id_q + i, own)
    forward_block(z, True)

    def rows_step_two():
        if nx == 1:
            return
        for cc in range(2):
            recv(row_slot(2 * left + cc), id_from_left + cc)
            recv(row_slot(2 * right + cc), id_from_right + cc)
        send(row_slot(2 * left), row_slot(2 * left), id_far_left, dev(z, y, right, c))
        send(row_slot(2 * right + 1), row_slot(2 * right + 1), id_far_right, dev(z, y, left, c))

    id_slice, id_proj, id_go = alloc("recv", NY), alloc("recv"), alloc("recv", NY)
    row_iota = lax.broadcasted_iota(jnp.int32, (HD, shards * cap), 0)

    def project():
        recv(row_slot(2 * x + sib), id_rows_sib)
        if nx > 1:
            opposite = (x + 2) % nx
            recv(row_slot(2 * opposite), id_far_left)
            recv(row_slot(2 * opposite + 1), id_far_right)
        lanes = lax.broadcasted_iota(jnp.int32, (1, shards * cap), 1)
        place = jnp.full((1, shards * cap), -1, jnp.int32)
        for i in range(shards):
            within = lanes - i * cap
            live = jnp.logical_and(within >= 0, within < counts[i])
            place = jnp.where(live, starts[i] + within, place)
        compact = (row_iota == place).astype(F32).astype(BF)
        block = buf["block"]
        block[...] = dot(compact, rows[...], 1, 0).astype(BF)
        for i in range(hz):
            for yy in range(NY):
                k = i * NY + yy
                buf["slice_out"][yy, :, i * HD : (i + 1) * HD] = block[:, k * HD : (k + 1) * HD]
        for yy in range(NY):
            buf["slice_out"][yy, :, hz * HD :] = block[:, dh:]
        weight_in.wait()
        recv(buf["weight"].at[sib], id_w)
        part = buf["proj_part"]
        part[sib] = dot(block[:, :dh], buf["weight"][sib], 1, 1)
        send(part.at[sib], buf["proj_in"], id_proj, dev_sib)
        part[c] = dot(block[:, :dh], buf["weight"][c], 1, 1)

    def out_gradient():
        recv(buf["proj_in"], id_proj)
        total = buf["proj_part"][c] + buf["proj_in"][...]
        buf["proj"][...] = total
        gate = buf["block"][:, dh:].astype(F32)
        for j in range(2):
            buf["go_out"][j] = (gate * total[:, j * HD : (j + 1) * HD]).astype(BF)
        for j in range(2):
            y_to = 2 * c + j
            for cc in range(2):
                own = jnp.logical_and(y_to == y, c == cc)
                send(buf["go_out"].at[j], buf["goh"].at[y], id_go + y, dev(z, y_to, x, cc), own)

                @pl.when(own)
                def _():
                    buf["goh"][y] = buf["go_out"][j]

        for dy in range(1, NY):
            y_to = (y + dy) % NY
            mine = pl.ds(pl.multiple_of(y * HD, HD), HD)
            send(
                buf["slice_out"].at[y_to],
                buf["slices"].at[mine, :],
                id_slice + y,
                dev(z, y_to, x, c),
            )
        buf["slices"][mine, :] = buf["slice_out"][y]

    for t in range(1, lay.far + 1):
        ring_recv(t)
        if t < lay.far:
            ring_send(t + 1)
        if t == 1:
            rows_step_two()
        if t == min(2, lay.far):
            project()
        if t == min(3, lay.far):
            out_gradient()
        forward_pair(t)

    id_soft = alloc("recv")
    send(soft, buf["soft_in"], id_soft, dev_sib)
    for i in range(NY):
        own = jnp.logical_and(c == half_y, y == i)
        recv(buf["goh"].at[i], id_go + i, own)
    recv(buf["soft_in"], id_soft)
    soft_in = buf["soft_in"]
    for i in range(NY):
        max_a, max_b = soft[i, HD : HD + 1, :], soft_in[i, HD : HD + 1, :]
        top = jnp.maximum(max_a, max_b)
        scale_a, scale_b = jnp.exp(max_a - top), jnp.exp(max_b - top)
        norm = soft[i, HD + 8 : HD + 9, :] * scale_a + soft_in[i, HD + 8 : HD + 9, :] * scale_b
        out_t = (soft[i, 0:HD, :] * scale_a + soft_in[i, 0:HD, :] * scale_b) / norm
        out = out_t.T.astype(BF)
        buf["outs"][y, i * HD : (i + 1) * HD, :] = out
        buf["lse"][i, 0:1, :] = top + jnp.log(norm)
        terms = out.astype(F32) * buf["goh"][i].astype(F32)
        buf["delta"][i, 0:1, :] = jnp.sum(terms.T, axis=0, keepdims=True)

    id_outs = alloc("recv", NY)
    for dy in range(1, NY):
        y_to = (y + dy) % NY
        send(buf["outs"].at[y], buf["outs"].at[y], id_outs + y, dev(z, y_to, x, c))

    def backward_block(b, diagonal):
        keys, values = buf["kk"][b], buf["vv"][b]
        for i in range(NY):
            queries, go = buf["qh"][i], buf["goh"][i]
            scores = dot(keys, queries, 1, 1) * factor
            weights = jnp.exp(scores - buf["lse"][i, 0:1, :])
            if diagonal:
                weights = jnp.where(allowed(i), weights, 0.0)
            grad_weights = dot(values, go, 1, 1)
            grad_scores = (weights * (grad_weights - buf["delta"][i, 0:1, :])).astype(BF)
            value_part = dot(weights.astype(BF), go, 1, 0)
            key_part = dot(grad_scores, queries, 1, 0)
            if i == 0:
                buf["dvp"][b] = value_part
                buf["dkp"][b] = key_part
            else:
                buf["dvp"][b] += value_part
                buf["dkp"][b] += key_part
            buf["dqt"][i] += dot(keys, grad_scores, 0, 0)

    def backward_pair(t):
        pl.when(z >= t)(lambda: backward_block((z + nz - t) % nz, False))
        if t <= nz - 1 - t:
            pl.when(z + t >= nz)(lambda: backward_block((z + t) % nz, False))

    hops = ((lay.far, lay.near), (lay.near, lay.far))
    id_kv = alloc("recv", 4 * (lay.far + 1))
    id_dw = alloc("recv", 4 * (lay.far + 1))

    def target(direction, d):
        return (z + nz - d) % nz if direction == 0 else (z + d) % nz

    def reduce_step(d, dw):
        for kind in range(2):
            for direction in range(2):
                n = hops[kind][direction]
                if d > n:
                    continue
                t = n - d
                b = target(direction, d)
                out, inc = (
                    (buf["dw_send"], buf["dw_recv"]) if dw else (buf["kv_send"], buf["kv_recv"])
                )
                base = (id_dw if dw else id_kv) + (2 * kind + direction) * (lay.far + 1)
                to = dev_down if direction == 0 else dev_up
                skip = b // hz != c if dw else None

                def value(kind=kind, direction=direction, t=t, b=b, inc=inc):
                    if dw:
                        mine = buf["dwp"][kind, b % hz]
                    else:
                        mine = (buf["dkp"] if kind == 0 else buf["dvp"])[b]
                    if t > 0:
                        mine = mine + inc[kind, direction, t - 1].astype(F32)
                    out[kind, direction, t] = mine.astype(BF)

                if t > 0:
                    recv(inc.at[kind, direction, t - 1], base + t - 1, skip)
                if skip is None:
                    value()
                else:
                    pl.when(jnp.logical_not(skip))(value)
                send(out.at[kind, direction, t], inc.at[kind, direction, t], base + t, to, skip)

    def reduce_last(dw):
        results = []
        skip = z // hz != c if dw else None
        for kind in range(2):
            for direction in range(2):
                n = hops[kind][direction]
                inc = buf["dw_recv"] if dw else buf["kv_recv"]
                base = (id_dw if dw else id_kv) + (2 * kind + direction) * (lay.far + 1)
                if n > 0:
                    recv(inc.at[kind, direction, n - 1], base + n - 1, skip)

        def value(kind):
            if dw:
                mine = buf["dwp"][kind, z % hz]
            else:
                mine = (buf["dkp"] if kind == 0 else buf["dvp"])[z]
            for direction in range(2):
                n = hops[kind][direction]
                inc = buf["dw_recv"] if dw else buf["kv_recv"]
                if n > 0:
                    mine = mine + inc[kind, direction, n - 1].astype(F32)
            return mine

        return value, skip

    id_router = alloc("recv", shards)

    def weight_gradient():
        for dy in range(1, NY):
            yy = (y + dy) % NY
            recv(buf["outs"].at[yy], id_outs + yy)
            recv(buf["slices"].at[pl.ds(pl.multiple_of(yy * HD, HD), HD), :], id_slice + yy)
        gate = buf["slices"][:, hz * HD :].astype(F32)
        for h in range(NY):
            buf["gated"][:, h * HD : (h + 1) * HD] = (gate * buf["outs"][h].astype(F32)).astype(BF)
        for i in range(hz):
            for kind in range(2):
                buf["dwp"][kind, i] = dot(
                    buf["slices"][:, i * HD : (i + 1) * HD],
                    buf["gated"][:, kind * 2 * HD : (kind + 1) * 2 * HD],
                    0,
                    0,
                )

    def router_send():
        mine = pl.ds(pl.multiple_of(y * HD, HD), HD)
        part = jnp.zeros((HD, HD), F32)
        for j in range(2):
            part = part + buf["outs"][2 * c + j, mine, :].astype(F32) * buf["proj"][
                :, j * HD : (j + 1) * HD
            ]
        row = jnp.sum(part.T, axis=0, keepdims=True)
        buf["router"][...] = jnp.broadcast_to(row, (8, HD))
        buf["router_in"][g] = jnp.broadcast_to(row, (8, HD))
        for dx in range(nx):
            for cc in range(2):
                if dx == 0 and cc == 1:
                    continue
                to = dev_sib if dx == 0 else dev(z, y, (x + dx) % nx, cc)
                send(buf["router"], buf["router_in"].at[g], id_router + g, to)

    def router_last():
        for dx in range(nx):
            for cc in range(2):
                if dx == 0 and cc == 1:
                    continue
                src = 2 * x + sib if dx == 0 else 2 * ((x + dx) % nx) + cc
                recv(buf["router_in"].at[src], id_router + src)
        total = buf["router_in"][0]
        for i in range(1, shards):
            total = total + buf["router_in"][i]
        token_row = lax.broadcasted_iota(jnp.int32, (HD, cap), 0)
        token_slot = lax.broadcasted_iota(jnp.int32, (HD, cap), 1)
        own = jnp.logical_and(token_row == own_start + token_slot, token_slot < own_count)
        spread = dot(own.astype(F32).astype(BF), pick_bf, 1, 0)
        placed = dot(total, spread, 1, 0, lax.Precision.HIGHEST)
        sig = 1.0 / (1.0 + jnp.exp(-logit_row))
        lg_ref[...] = placed[0:1, :] * sig * (1.0 - sig)

    id_kv_fin, id_dq = alloc("recv", 4), alloc("recv", 4)
    id_dw_fin = alloc("recv")

    def send_key_value_grads():
        value, _ = reduce_last(False)
        for kind in range(2):
            final = value(kind)
            if kind == 0:
                final = final * factor
            for j in range(2):
                buf["kv_fin"][kind, j] = final[j * HD : (j + 1) * HD, :].astype(BF)
        side = y % 2
        for kind in range(2):
            for j in range(2):
                y_to = 2 * c + j
                own = jnp.logical_and(y_to == y, half_y == c)
                send(
                    buf["kv_fin"].at[kind, j],
                    buf["kv_land"].at[kind, side],
                    id_kv_fin + 2 * kind + side,
                    dev(z, y_to, x, half_y),
                    own,
                )

                @pl.when(own)
                def _():
                    buf["kv_land"][kind, side] = buf["kv_fin"][kind, j]

    def send_query_grads():
        side = y % 2
        for i in range(NY):
            buf["dq_out"][i] = (buf["dqt"][i].T * factor).astype(BF)
            own = jnp.logical_and(y == i, half_y == c)
            send(
                buf["dq_out"].at[i],
                buf["dq_land"].at[side, c],
                id_dq + 2 * side + c,
                dev(z, i, x, half_y),
                own,
            )

            @pl.when(own)
            def _():
                buf["dq_land"][side, c] = buf["dq_out"][i]

    dw_delay = 2
    for d in range(lay.far, -1, -1):
        if d > 0:
            backward_pair(d)
            reduce_step(d, False)
        else:
            backward_block(z, True)
            send_query_grads()
        if d == lay.far - 1 or lay.far == 1 and d == 0:
            weight_gradient()
            router_send()
        if d + dw_delay - 1 <= lay.far and d + dw_delay - 1 > 0 and lay.far > 1:
            reduce_step(d + dw_delay - 1, True)
    if lay.far == 1:
        reduce_step(1, True)
    send_key_value_grads()

    value, skip = reduce_last(True)

    @pl.when(jnp.logical_not(skip))
    def _():
        for kind in range(2):
            buf["dw_fin"][kind] = value(kind)

    holder = jnp.logical_not(skip)
    send(buf["dw_fin"].at[sib], buf["dw_land"], id_dw_fin, dev_sib, skip)
    router_last()

    for j in range(2):
        for cc in range(2):
            own = jnp.logical_and(y == 2 * c + j, c == cc)
            recv(buf["dq_land"].at[j, cc], id_dq + 2 * j + cc, own)
        dq_ref[:, j * HD : (j + 1) * HD] = (
            buf["dq_land"][j, 0].astype(F32) + buf["dq_land"][j, 1].astype(F32)
        ).astype(BF)
    for kind, ref in ((0, dk_ref), (1, dv_ref)):
        for j in range(2):
            own = jnp.logical_and(y == 2 * c + j, half_y == c)
            recv(buf["kv_land"].at[kind, j], id_kv_fin + 2 * kind + j, own)
            ref[:, j * HD : (j + 1) * HD] = buf["kv_land"][kind, j]

    recv(buf["dw_land"], id_dw_fin, holder)

    @pl.when(holder)
    def _():
        dw_ref[...] = buf["dw_fin"][c]

    @pl.when(skip)
    def _():
        dw_ref[...] = buf["dw_land"][...]

    for unless, copy in sent:
        if unless is None:
            copy.wait_send()
        else:
            pl.when(jnp.logical_not(unless))(lambda: copy.wait_send())

    lay.used = dict(counter)


SEMS = 160


def shards_fn(nz, nx):
    def run(grad, logit, index, count, weight, q, k, v):
        lay = Layout(nz, nx, grad.shape[0], index.shape[0], grad.shape[1])
        scratch = lay.scratch()
        names = list(scratch)
        any_ = pl.BlockSpec(memory_space=pl.ANY)
        smem = pl.BlockSpec(memory_space=pltpu.SMEM)
        vmem = pl.BlockSpec(memory_space=pltpu.VMEM)

        def kernel(*refs):
            fused(lay, names, *refs)

        out = pl.pallas_call(
            kernel,
            out_shape=(
                jax.ShapeDtypeStruct(q.shape, BF),
                jax.ShapeDtypeStruct(q.shape, BF),
                jax.ShapeDtypeStruct(q.shape, BF),
                jax.ShapeDtypeStruct((HD, q.shape[1]), F32),
                jax.ShapeDtypeStruct((1, logit.shape[0]), F32),
            ),
            in_specs=[any_, vmem, smem, smem, any_, any_, any_, any_],
            out_specs=(vmem,) * 5,
            scratch_shapes=list(scratch.values())
            + [
                pltpu.SemaphoreType.DMA((SEMS,)),
                pltpu.SemaphoreType.DMA((SEMS,)),
                pltpu.SemaphoreType.DMA((16,)),
            ],
            compiler_params=pltpu.CompilerParams(
                collective_id=0, has_side_effects=True, vmem_limit_bytes=48 * 1024 * 1024
            ),
            name="routed_backward",
        )(grad, logit.reshape(1, -1), index, count, weight, q, k, v)
        return (*out[:4], out[4].reshape(-1))

    return run


def solution(mesh):
    nz = mesh.shape["seq"] // NY
    nx = mesh.shape["grp"] // 2
    placed = (
        P(("seq", "grp"), None),
        P(("seq", "grp")),
        P(("seq", "grp")),
        P(),
        P("grp", None),
        P("seq", "grp"),
        P("seq", "grp"),
        P("seq", "grp"),
    )
    return jax.shard_map(
        shards_fn(nz, nx),
        mesh=mesh,
        in_specs=placed,
        out_specs=(
            P("seq", "grp"),
            P("seq", "grp"),
            P("seq", "grp"),
            P("seq", "grp"),
            P(("seq", "grp")),
        ),
        check_vma=False,
    )
```

time: 926 us -> 77.7 us (0.08)
  waiting for transfers between devices: 822 us -> 0 us
  Pallas kernels: 0 us -> 66.4 us
  blocking collectives: 27.8 us -> 0 us
  other arithmetic: 18 us -> 0 us
  between operations: 15.7 us -> 0.66 us
  local copies, waits for them, and re-layouts: 24.7 us -> 10.4 us
  matrix products: 10.4 us -> 0 us
    reduce_scatter x3 -> x0, waiting for transfers between devices: 650 us -> none  [the longest x1 218 us: shards(): lax.psum_scatter(value_acc.reshape(-1, local_cols).astype(jnp.bfloat16),...]
    all_gather x3 -> x0, waiting for transfers between devices: 172 us -> none  [the longest x1 75.5 us: shards(): lax.all_gather(value_rows, 'seq', axis=0, tiled=True)]
    pallas_call x0 -> x1, Pallas kernels: none -> 66.4 us  [run(): pl.pallas_call(kernel, out_shape=(jax.ShapeDtypeStruct(q.shape, BF), jax....]
    unnamed x2 -> x0, blocking collectives: 27.8 us -> none
    convert_element_type x8 -> x0, other arithmetic: 12.1 us -> none  [the longest x1 3.78 us: shards(): key_acc.reshape(-1, local_cols).astype(jnp.bfloat16)]
    dot_general x9 -> x0, matrix products: 10.4 us -> none  [the longest x1 2.13 us: shards(): lax.dot_general(grad_block, gated_out, (((0,), (0,)), ((), ())), preferre...]
  transfers between devices with their start and end apart: 6 -> 0, of which waited for: 6 -> 0; matrix products, arithmetic and copies ran while one was open for 4% -> 0% of each run, Pallas kernels for 0% -> 0%
where the time goes in v1:
time: 77.7 us; the launch traced here: 77.4 us
  Pallas kernels  66.4 us (85%)
  local copies, waits for them, and re-layouts  10.4 us (13%)
    pallas_call x1, Pallas kernels, run(): pl.pallas_call(kernel, out_shape=(jax.ShapeDtypeStruct(q.shape, BF), jax....  66.4 us
    unnamed x21, local copies, waits for them, and re-layouts  10.4 us

profile of v1, /device:TPU:1, one launch (start us, length us, event | category | flops | bytes accessed | tf_op | source)
XLA Modules:
  0.0 77.4 jit_solution(4260263992703341945)
XLA Ops:
  0.6 0.0 copy-start
  0.6 1.6 %copy-done = bf16[256,4096]{1,0:T(8,128)(2,1)S(1)} copy-done((bf16[256,4096]{1,0:T(8,128)(2,1)S(1)}, bf16[256,4096]{1,0:T(8,128)(2,1)}, u32[]{:S(2)}) %copy-start) | copy-done | bytes 2097176
  2.2 0.0 copy-start.1
  2.2 1.2 %copy-done.1 = bf16[128,4096]{1,0:T(8,128)(2,1)S(1)} copy-done((bf16[128,4096]{1,0:T(8,128)(2,1)S(1)}, bf16[128,4096]{1,0:T(8,128)(2,1)}, u32[]{:S(2)}) %copy-start.1) | copy-done | bytes 1048600
  3.5 0.0 copy-start.2
  3.5 0.8 %copy-done.2 = bf16[128,256]{1,0:T(8,128)(2,1)S(1)} copy-done((bf16[128,256]{1,0:T(8,128)(2,1)S(1)}, bf16[128,256]{1,0:T(8,128)(2,1)}, u32[]{:S(2)}) %copy-start.2) | copy-done | bytes 65560
  4.3 0.0 copy-start.3
  4.3 0.8 %copy-done.3 = bf16[128,256]{1,0:T(8,128)(2,1)S(1)} copy-done((bf16[128,256]{1,0:T(8,128)(2,1)S(1)}, bf16[128,256]{1,0:T(8,128)(2,1)}, u32[]{:S(2)}) %copy-start.3) | copy-done | bytes 65560
  5.1 0.0 copy-start.4
  5.1 0.8 %copy-done.4 = bf16[128,256]{1,0:T(8,128)(2,1)S(1)} copy-done((bf16[128,256]{1,0:T(8,128)(2,1)S(1)}, bf16[128,256]{1,0:T(8,128)(2,1)}, u32[]{:S(2)}) %copy-start.4) | copy-done | bytes 65560
  6.0 0.0 copy-start.5
  6.0 0.7 copy-done.5
  6.7 0.0 copy-start.6
  6.7 0.7 copy-done.6
  7.3 0.0 copy-start.7
  7.3 0.7 copy-done.7
  8.0 66.4 %routed_backward.1 = (bf16[128,256]{1,0:T(8,128)(2,1)S(1)}, bf16[128,256]{1,0:T(8,128)(2,1)S(1)}, bf16[128,256]{1,0:T(8,128)(2,1)S(1)}, f32[128,256]{1,0:T(8,128)S(1)}, f32[1,128]{1,0:T(1,128)S(1)}) custom-call(bf16[128,4096]{1,0:T(8,128)(2,1)S(1)} %copy-done.1, f32[1,128]{1,0:T(1,128)S(1)} %bitcast.2, s32[32]{0:T(128)S(1)} %copy-done.7, s32[256]{0:T(256)S(1)} %copy-done.5, ...), custom_call_target="tpu_custom_call" | custom-call | tf_op jit(solution)/shard_map/routed_backward/pallas_call | solution.py:668
  74.3 0.6 copy.18
  75.0 0.6 copy.19
  75.6 0.6 copy.20
  76.2 0.7 copy.21
  76.9 0.5 copy.22
Async XLA Ops:
  0.6 1.6 %copy-start = (bf16[256,4096]{1,0:T(8,128)(2,1)S(1)}, bf16[256,4096]{1,0:T(8,128)(2,1)}, u32[]{:S(2)}) copy-start(bf16[256,4096]{1,0:T(8,128)(2,1)} %refs_4_.1) | copy-start | bytes 6291460
  2.2 1.2 %copy-start.1 = (bf16[128,4096]{1,0:T(8,128)(2,1)S(1)}, bf16[128,4096]{1,0:T(8,128)(2,1)}, u32[]{:S(2)}) copy-start(bf16[128,4096]{1,0:T(8,128)(2,1)} %refs_0_.1) | copy-start | bytes 3145732
  3.5 0.8 %copy-start.2 = (bf16[128,256]{1,0:T(8,128)(2,1)S(1)}, bf16[128,256]{1,0:T(8,128)(2,1)}, u32[]{:S(2)}) copy-start(bf16[128,256]{1,0:T(8,128)(2,1)} %refs_5_.1) | copy-start | bytes 196612
  4.3 0.8 %copy-start.3 = (bf16[128,256]{1,0:T(8,128)(2,1)S(1)}, bf16[128,256]{1,0:T(8,128)(2,1)}, u32[]{:S(2)}) copy-start(bf16[128,256]{1,0:T(8,128)(2,1)} %refs_6_.1) | copy-start | bytes 196612
  5.1 0.8 %copy-start.4 = (bf16[128,256]{1,0:T(8,128)(2,1)S(1)}, bf16[128,256]{1,0:T(8,128)(2,1)}, u32[]{:S(2)}) copy-start(bf16[128,256]{1,0:T(8,128)(2,1)} %refs_7_.1) | copy-start | bytes 196612
  6.0 0.7 copy-start.5
  6.7 0.7 copy-start.6
  7.3 0.7 copy-start.7

commit v2 on v1

--- a/solution.py
+++ b/solution.py
@@ -37,11 +37,11 @@
             picked=v((2, cap, dh + HD), BF),
             rows=v((2 * nx * cap, dh + HD), BF),
             block=v((HD, dh + HD), BF),
-            slice_out=v((NY, HD, (hz + 1) * HD), BF),
-            slices=v((NY * HD, (hz + 1) * HD), BF),
+            slice_out=v((NY, HD, hz * HD), BF),
+            slices=v((NY * HD, hz * HD), BF),
+            gates=v((NY, 8, HD), F32),
             proj_part=v((2, HD, 2 * HD), F32),
             proj_in=v((HD, 2 * HD), F32),
-            proj=v((HD, 2 * HD), F32),
             go_out=v((2, HD, HD), BF),
             qh=v((NY, HD, HD), BF),
             goh=v((NY, HD, HD), BF),
@@ -51,8 +51,7 @@
             soft_in=v((NY, HD + 16, HD), F32),
             lse=v((NY, 8, HD), F32),
             delta=v((NY, 8, HD), F32),
-            outs=v((NY, NY * HD, HD), BF),
-            gated=v((NY * HD, NY * HD), BF),
+            outs=v((NY * HD, NY * HD), BF),
             dqt=v((NY, HD, HD), F32),
             dkp=v((nz, 2 * HD, HD), F32),
             dvp=v((nz, 2 * HD, HD), F32),
@@ -62,22 +61,20 @@
             dw_send=v((2, 2, steps, HD, 2 * HD), BF),
             dw_recv=v((2, 2, steps, HD, 2 * HD), BF),
             kv_fin=v((2, 2, HD, HD), BF),
-            kv_land=v((2, 2, HD, HD), BF),
             dq_out=v((NY, HD, HD), BF),
-            dq_land=v((2, 2, HD, HD), BF),
             dw_fin=v((2, HD, 2 * HD), F32),
-            dw_land=v((HD, 2 * HD), F32),
-            router=v((8, HD), F32),
-            router_in=v((2 * nx, 8, HD), F32),
+            router_out=v((NY, 8, HD), F32),
+            router_y=v((NY, 8, HD), F32),
+            router_x=v((nx, 8, HD), F32),
         )
         return names
 
 
 def fused(lay, names, *refs):
     (g_ref, logit_ref, idx_ref, cnt_ref, w_ref, q_ref, k_ref, v_ref) = refs[:8]
-    (dq_ref, dk_ref, dv_ref, dw_ref, lg_ref) = refs[8:13]
-    buf = dict(zip(names, refs[13 : 13 + len(names)]))
-    send_sems, recv_sems, local_sems = refs[13 + len(names) :]
+    (dq_land, kv_land, dw_land, lg_ref) = refs[8:12]
+    buf = dict(zip(names, refs[12 : 12 + len(names)]))
+    send_sems, recv_sems, local_sems = refs[12 + len(names) :]
     nz, nx, cap, dh, hz = lay.nz, lay.nx, lay.cap, lay.dh, lay.hz
     shards = 2 * nx
     factor = HD ** (-0.5)
@@ -130,6 +127,13 @@
             copy.wait_recv()
         else:
             pl.when(jnp.logical_not(unless))(lambda: copy.wait_recv())
+
+    local = []
+
+    def keep(src, dst, own):
+        copy = pltpu.make_async_copy(src, dst, local_sems.at[alloc("local")])
+        pl.when(own)(lambda: copy.start())
+        local.append((own, copy))
 
     grads_in = pltpu.make_async_copy(g_ref, buf["grads"], local_sems.at[alloc("local")])
     grads_in.start()
@@ -220,13 +224,14 @@
         return rows.at[pl.ds(pl.multiple_of(shard * cap, cap), cap), :]
 
     id_rows_sib = alloc("recv")
-    id_from_left, id_from_right = alloc("recv", 2), alloc("recv", 2)
+    id_step_one = alloc("recv", 4)
+    id_from_left, id_from_right = id_step_one, id_step_one + 2
     id_far_left, id_far_right = alloc("recv"), alloc("recv")
     send(buf["picked"].at[sib], row_slot(g), id_rows_sib, dev_sib)
     if nx > 1:
-        for h in range(2):
-            send(buf["picked"].at[h], row_slot(g), id_from_left + c, dev(z, y, right, h))
-            send(buf["picked"].at[h], row_slot(g), id_from_right + c, dev(z, y, left, h))
+        for to, side in ((jnp.where(c == 0, right, left), c), (jnp.where(c == 0, left, right), sib)):
+            for h in range(2):
+                send(buf["picked"].at[h], row_slot(g), id_step_one + 2 * side + c, dev(z, y, to, h))
     rows[pl.ds(pl.multiple_of(g * cap, cap), cap), :] = buf["picked"][c]
 
     buf["dkp"][...] = jnp.zeros_like(buf["dkp"])
@@ -237,7 +242,6 @@
     for i in range(NY):
         soft[i, HD : HD + 8, :] = jnp.full((8, HD), NEG, F32)
 
-    kv_own = pl.ds(pl.multiple_of(0, HD), HD)
     for j in range(2):
         own = jnp.logical_and(c == half_y, y == 2 * c + j)
         part = slice(j * HD, (j + 1) * HD)
@@ -246,27 +250,26 @@
     for own, copy in own_copies:
         pl.when(own)(lambda: copy.wait())
 
-    ring = (("kk", lay.far, lay.near), ("vv", lay.near, lay.far))
-    id_up = {n: alloc("recv", lay.far + 1) for n in ("kk", "vv")}
-    id_down = {n: alloc("recv", lay.far + 1) for n in ("kk", "vv")}
-
-    def ring_send(t):
-        for name, n_up, n_down in ring:
-            if t <= n_up:
-                b = (z + nz - t + 1) % nz
-                send(buf[name].at[b], buf[name].at[b], id_up[name] + t, dev_up)
-            if t <= n_down:
-                b = (z + t - 1) % nz
-                send(buf[name].at[b], buf[name].at[b], id_down[name] + t, dev_down)
-
-    def ring_recv(t):
-        for name, n_up, n_down in ring:
-            if t <= n_up:
-                recv(buf[name].at[(z + nz - t) % nz], id_up[name] + t)
-            if t <= n_down:
-                recv(buf[name].at[(z + t) % nz], id_down[name] + t)
-
-    ring_send(1)
+    halves = (slice(0, HD), slice(HD, 2 * HD))
+    ring = [
+        (name, half, n_up, n_down)
+        for name, n_up, n_down in (("kk", lay.far, lay.near), ("vv", lay.near, lay.far))
+        for half in range(2)
+    ]
+    id_ring = {(name, half): alloc("recv", 2 * (lay.far + 1)) for name, half, _, _ in ring}
+
+    def ring_step(t):
+        for name, half, n_up, n_down in ring:
+            base = id_ring[name, half]
+            for side, hops in ((0, n_up), (1, n_down)):
+                b = (z + nz - t) % nz if side == 0 else (z + t) % nz
+                ref = buf[name].at[b, halves[half], :]
+                if 1 <= t <= hops:
+                    recv(ref, base + 2 * t + side)
+                if t + 1 <= hops:
+                    send(ref, ref, base + 2 * (t + 1) + side, dev_up if side == 0 else dev_down)
+
+    ring_step(0)
 
     def allowed(i):
         key = c * 2 * HD + lax.broadcasted_iota(jnp.int32, (2 * HD, HD), 0)
@@ -308,6 +311,7 @@
         send(row_slot(2 * right + 1), row_slot(2 * right + 1), id_far_right, dev(z, y, left, c))
 
     id_slice, id_proj, id_go = alloc("recv", NY), alloc("recv"), alloc("recv", NY)
+    id_gate = alloc("recv", NY)
     row_iota = lax.broadcasted_iota(jnp.int32, (HD, shards * cap), 0)
 
     def project():
@@ -329,8 +333,11 @@
             for yy in range(NY):
                 k = i * NY + yy
                 buf["slice_out"][yy, :, i * HD : (i + 1) * HD] = block[:, k * HD : (k + 1) * HD]
-        for yy in range(NY):
-            buf["slice_out"][yy, :, hz * HD :] = block[:, dh:]
+        gate_rows = block[:, dh:].astype(F32).T
+        buf["gates"][y] = gate_rows[0:8, :]
+        for dy in range(1, NY):
+            y_to = (y + dy) % NY
+            send(buf["gates"].at[y], buf["gates"].at[y], id_gate + y, dev(z, y_to, x, c))
         weight_in.wait()
         recv(buf["weight"].at[sib], id_w)
         part = buf["proj_part"]
@@ -341,7 +348,6 @@
     def out_gradient():
         recv(buf["proj_in"], id_proj)
         total = buf["proj_part"][c] + buf["proj_in"][...]
-        buf["proj"][...] = total
         gate = buf["block"][:, dh:].astype(F32)
         for j in range(2):
             buf["go_out"][j] = (gate * total[:, j * HD : (j + 1) * HD]).astype(BF)
@@ -367,9 +373,7 @@
         buf["slices"][mine, :] = buf["slice_out"][y]
 
     for t in range(1, lay.far + 1):
-        ring_recv(t)
-        if t < lay.far:
-            ring_send(t + 1)
+        ring_step(t)
         if t == 1:
             rows_step_two()
         if t == min(2, lay.far):
@@ -383,7 +387,11 @@
     for i in range(NY):
         own = jnp.logical_and(c == half_y, y == i)
         recv(buf["goh"].at[i], id_go + i, own)
+    for dy in range(1, NY):
+        yy = (y + dy) % NY
+        recv(buf["gates"].at[yy], id_gate + yy)
     recv(buf["soft_in"], id_soft)
+    head_cols = pl.ds(pl.multiple_of(y * HD, HD), HD)
     soft_in = buf["soft_in"]
     for i in range(NY):
         max_a, max_b = soft[i, HD : HD + 1, :], soft_in[i, HD : HD + 1, :]
@@ -391,16 +399,28 @@
         scale_a, scale_b = jnp.exp(max_a - top), jnp.exp(max_b - top)
         norm = soft[i, HD + 8 : HD + 9, :] * scale_a + soft_in[i, HD + 8 : HD + 9, :] * scale_b
         out_t = (soft[i, 0:HD, :] * scale_a + soft_in[i, 0:HD, :] * scale_b) / norm
-        out = out_t.T.astype(BF)
-        buf["outs"][y, i * HD : (i + 1) * HD, :] = out
+        out_t = out_t.astype(BF).astype(F32)
+        gate_row = buf["gates"][i, 0:1, :]
+        buf["outs"][i * HD : (i + 1) * HD, head_cols] = (gate_row * out_t).T.astype(BF)
         buf["lse"][i, 0:1, :] = top + jnp.log(norm)
-        terms = out.astype(F32) * buf["goh"][i].astype(F32)
-        buf["delta"][i, 0:1, :] = jnp.sum(terms.T, axis=0, keepdims=True)
-
-    id_outs = alloc("recv", NY)
+        delta = jnp.sum(out_t * buf["goh"][i].astype(F32).T, axis=0, keepdims=True)
+        buf["delta"][i, 0:1, :] = delta
+        buf["router_out"][i] = jnp.broadcast_to(delta / gate_row, (8, HD))
+
+    id_outs, id_outs_sib, id_router_y = alloc("recv", NY), alloc("recv", NY), alloc("recv", NY)
+
+    def out_part(head, core):
+        return buf["outs"].at[
+            pl.ds(pl.multiple_of(core * 2 * HD, HD), 2 * HD),
+            pl.ds(pl.multiple_of(head * HD, HD), HD),
+        ]
+
     for dy in range(1, NY):
         y_to = (y + dy) % NY
-        send(buf["outs"].at[y], buf["outs"].at[y], id_outs + y, dev(z, y_to, x, c))
+        to = dev(z, y_to, x, c)
+        send(out_part(y, c), out_part(y, c), id_outs + y, to)
+        send(buf["router_out"].at[y_to], buf["router_y"].at[y], id_router_y + y, to)
+    buf["router_y"][y] = buf["router_out"][y]
 
     def backward_block(b, diagonal):
         keys, values = buf["kk"][b], buf["vv"][b]
@@ -428,115 +448,119 @@
             pl.when(z + t >= nz)(lambda: backward_block((z + t) % nz, False))
 
     hops = ((lay.far, lay.near), (lay.near, lay.far))
-    id_kv = alloc("recv", 4 * (lay.far + 1))
+    id_kv = alloc("recv", 8 * (lay.far + 1))
     id_dw = alloc("recv", 4 * (lay.far + 1))
 
     def target(direction, d):
         return (z + nz - d) % nz if direction == 0 else (z + d) % nz
 
+    def chain_id(dw, kind, direction, part):
+        steps = lay.far + 1
+        if dw:
+            return id_dw + (2 * kind + direction) * steps
+        return id_kv + (4 * (part.start // HD) + 2 * kind + direction) * steps
+
     def reduce_step(d, dw):
         for kind in range(2):
+            for part in halves if not dw else (slice(0, HD),):
+                for direction in range(2):
+                    n = hops[kind][direction]
+                    if d > n:
+                        continue
+                    t = n - d
+                    b = target(direction, d)
+                    base = chain_id(dw, kind, direction, part)
+                    to = dev_down if direction == 0 else dev_up
+                    skip = b // hz != c if dw else None
+                    if dw:
+                        mine, out, inc = buf["dwp"].at[kind, b % hz], buf["dw_send"], buf["dw_recv"]
+                    else:
+                        mine = (buf["dkp"] if kind == 0 else buf["dvp"]).at[b, part, :]
+                        out, inc = buf["kv_send"], buf["kv_recv"]
+
+                    def value():
+                        total = mine[...]
+                        if t > 0:
+                            total = total + inc[kind, direction, t - 1, part, :].astype(F32)
+                        out[kind, direction, t, part, :] = total.astype(BF)
+
+                    if t > 0:
+                        recv(inc.at[kind, direction, t - 1, part, :], base + t - 1, skip)
+                    if skip is None:
+                        value()
+                    else:
+                        pl.when(jnp.logical_not(skip))(value)
+                    send(
+                        out.at[kind, direction, t, part, :],
+                        inc.at[kind, direction, t, part, :],
+                        base + t,
+                        to,
+                        skip,
+                    )
+
+    def reduce_last(dw, kind, part, skip=None):
+        inc = buf["dw_recv"] if dw else buf["kv_recv"]
+        for direction in range(2):
+            n = hops[kind][direction]
+            if n > 0:
+                base = chain_id(dw, kind, direction, part)
+                recv(inc.at[kind, direction, n - 1, part, :], base + n - 1, skip)
+
+        def value():
+            if dw:
+                total = buf["dwp"][kind, z % hz]
+            else:
+                total = (buf["dkp"] if kind == 0 else buf["dvp"])[z, part, :]
             for direction in range(2):
                 n = hops[kind][direction]
-                if d > n:
-                    continue
-                t = n - d
-                b = target(direction, d)
-                out, inc = (
-                    (buf["dw_send"], buf["dw_recv"]) if dw else (buf["kv_send"], buf["kv_recv"])
-                )
-                base = (id_dw if dw else id_kv) + (2 * kind + direction) * (lay.far + 1)
-                to = dev_down if direction == 0 else dev_up
-                skip = b // hz != c if dw else None
-
-                def value(kind=kind, direction=direction, t=t, b=b, inc=inc):
-                    if dw:
-                        mine = buf["dwp"][kind, b % hz]
-                    else:
-                        mine = (buf["dkp"] if kind == 0 else buf["dvp"])[b]
-                    if t > 0:
-                        mine = mine + inc[kind, direction, t - 1].astype(F32)
-                    out[kind, direction, t] = mine.astype(BF)
-
-                if t > 0:
-                    recv(inc.at[kind, direction, t - 1], base + t - 1, skip)
-                if skip is None:
-                    value()
-                else:
-                    pl.when(jnp.logical_not(skip))(value)
-                send(out.at[kind, direction, t], inc.at[kind, direction, t], base + t, to, skip)
-
-    def reduce_last(dw):
-        results = []
-        skip = z // hz != c if dw else None
-        for kind in range(2):
-            for direction in range(2):
-                n = hops[kind][direction]
-                inc = buf["dw_recv"] if dw else buf["kv_recv"]
-                base = (id_dw if dw else id_kv) + (2 * kind + direction) * (lay.far + 1)
                 if n > 0:
-                    recv(inc.at[kind, direction, n - 1], base + n - 1, skip)
-
-        def value(kind):
-            if dw:
-                mine = buf["dwp"][kind, z % hz]
-            else:
-                mine = (buf["dkp"] if kind == 0 else buf["dvp"])[z]
-            for direction in range(2):
-                n = hops[kind][direction]
-                inc = buf["dw_recv"] if dw else buf["kv_recv"]
-                if n > 0:
-                    mine = mine + inc[kind, direction, n - 1].astype(F32)
-            return mine
-
-        return value, skip
-
-    id_router = alloc("recv", shards)
+                    total = total + inc[kind, direction, n - 1, part, :].astype(F32)
+            return total
+
+        return value
+
+    def share_outs():
+        for dy in range(1, NY):
+            yy = (y + dy) % NY
+            recv(out_part(yy, c), id_outs + yy)
+            send(out_part(yy, c), out_part(yy, c), id_outs_sib + yy, dev_sib)
 
     def weight_gradient():
         for dy in range(1, NY):
             yy = (y + dy) % NY
-            recv(buf["outs"].at[yy], id_outs + yy)
             recv(buf["slices"].at[pl.ds(pl.multiple_of(yy * HD, HD), HD), :], id_slice + yy)
-        gate = buf["slices"][:, hz * HD :].astype(F32)
-        for h in range(NY):
-            buf["gated"][:, h * HD : (h + 1) * HD] = (gate * buf["outs"][h].astype(F32)).astype(BF)
+            recv(out_part(yy, sib), id_outs_sib + yy)
         for i in range(hz):
             for kind in range(2):
                 buf["dwp"][kind, i] = dot(
                     buf["slices"][:, i * HD : (i + 1) * HD],
-                    buf["gated"][:, kind * 2 * HD : (kind + 1) * 2 * HD],
+                    buf["outs"][:, kind * 2 * HD : (kind + 1) * 2 * HD],
                     0,
                     0,
                 )
 
+    id_router_x = alloc("recv", nx)
+
     def router_send():
-        mine = pl.ds(pl.multiple_of(y * HD, HD), HD)
-        part = jnp.zeros((HD, HD), F32)
-        for j in range(2):
-            part = part + buf["outs"][2 * c + j, mine, :].astype(F32) * buf["proj"][
-                :, j * HD : (j + 1) * HD
-            ]
-        row = jnp.sum(part.T, axis=0, keepdims=True)
-        buf["router"][...] = jnp.broadcast_to(row, (8, HD))
-        buf["router_in"][g] = jnp.broadcast_to(row, (8, HD))
-        for dx in range(nx):
-            for cc in range(2):
-                if dx == 0 and cc == 1:
-                    continue
-                to = dev_sib if dx == 0 else dev(z, y, (x + dx) % nx, cc)
-                send(buf["router"], buf["router_in"].at[g], id_router + g, to)
+        for dy in range(1, NY):
+            yy = (y + dy) % NY
+            recv(buf["router_y"].at[yy], id_router_y + yy)
+        total = buf["router_y"][0]
+        for i in range(1, NY):
+            total = total + buf["router_y"][i]
+        buf["router_x"][x] = total
+        for dx in range(1, nx):
+            x_to = (x + dx) % nx
+            ref = buf["router_x"].at[x]
+            send(ref, ref, id_router_x + x, dev(z, y, x_to, c))
 
     def router_last():
-        for dx in range(nx):
-            for cc in range(2):
-                if dx == 0 and cc == 1:
-                    continue
-                src = 2 * x + sib if dx == 0 else 2 * ((x + dx) % nx) + cc
-                recv(buf["router_in"].at[src], id_router + src)
-        total = buf["router_in"][0]
-        for i in range(1, shards):
-            total = total + buf["router_in"][i]
+        for dx in range(1, nx):
+            xx = (x + dx) % nx
+            recv(buf["router_x"].at[xx], id_router_x + xx)
+        total = buf["router_x"][0]
+        for i in range(1, nx):
+            total = total + buf["router_x"][i]
         token_row = lax.broadcasted_iota(jnp.int32, (HD, cap), 0)
         token_slot = lax.broadcasted_iota(jnp.int32, (HD, cap), 1)
         own = jnp.logical_and(token_row == own_start + token_slot, token_slot < own_count)
@@ -547,110 +571,92 @@
 
     id_kv_fin, id_dq = alloc("recv", 4), alloc("recv", 4)
     id_dw_fin = alloc("recv")
+    side = y % 2
 
     def send_key_value_grads():
-        value, _ = reduce_last(False)
-        for kind in range(2):
-            final = value(kind)
-            if kind == 0:
-                final = final * factor
-            for j in range(2):
-                buf["kv_fin"][kind, j] = final[j * HD : (j + 1) * HD, :].astype(BF)
-        side = y % 2
         for kind in range(2):
             for j in range(2):
+                final = reduce_last(False, kind, halves[j])()
+                if kind == 0:
+                    final = final * factor
+                buf["kv_fin"][kind, j] = final.astype(BF)
                 y_to = 2 * c + j
                 own = jnp.logical_and(y_to == y, half_y == c)
-                send(
-                    buf["kv_fin"].at[kind, j],
-                    buf["kv_land"].at[kind, side],
-                    id_kv_fin + 2 * kind + side,
-                    dev(z, y_to, x, half_y),
-                    own,
-                )
-
-                @pl.when(own)
-                def _():
-                    buf["kv_land"][kind, side] = buf["kv_fin"][kind, j]
+                src, dst = buf["kv_fin"].at[kind, j], kv_land.at[kind, side]
+                send(src, dst, id_kv_fin + 2 * kind + side, dev(z, y_to, x, half_y), own)
+                keep(src, dst, own)
 
     def send_query_grads():
-        side = y % 2
         for i in range(NY):
             buf["dq_out"][i] = (buf["dqt"][i].T * factor).astype(BF)
             own = jnp.logical_and(y == i, half_y == c)
-            send(
-                buf["dq_out"].at[i],
-                buf["dq_land"].at[side, c],
-                id_dq + 2 * side + c,
-                dev(z, i, x, half_y),
-                own,
-            )
-
-            @pl.when(own)
-            def _():
-                buf["dq_land"][side, c] = buf["dq_out"][i]
-
-    dw_delay = 2
-    for d in range(lay.far, -1, -1):
-        if d > 0:
-            backward_pair(d)
-            reduce_step(d, False)
-        else:
-            backward_block(z, True)
-            send_query_grads()
-        if d == lay.far - 1 or lay.far == 1 and d == 0:
+            src, dst = buf["dq_out"].at[i], dq_land.at[side, c]
+            send(src, dst, id_dq + 2 * side + c, dev(z, i, x, half_y), own)
+            keep(src, dst, own)
+
+    late = min(2, lay.far)
+    for d in range(lay.far, 0, -1):
+        backward_pair(d)
+        reduce_step(d, False)
+        if d == lay.far:
+            share_outs()
+        if d == late:
             weight_gradient()
             router_send()
-        if d + dw_delay - 1 <= lay.far and d + dw_delay - 1 > 0 and lay.far > 1:
-            reduce_step(d + dw_delay - 1, True)
-    if lay.far == 1:
+            reduce_step(lay.far, True)
+        elif d < late:
+            reduce_step(lay.far - late + d, True)
+    backward_block(z, True)
+    send_query_grads()
+    for d in range(lay.far - late, 1, -1):
+        reduce_step(d, True)
+    send_key_value_grads()
+    if lay.far - late >= 1:
         reduce_step(1, True)
-    send_key_value_grads()
-
-    value, skip = reduce_last(True)
-
-    @pl.when(jnp.logical_not(skip))
-    def _():
-        for kind in range(2):
-            buf["dw_fin"][kind] = value(kind)
-
+    router_last()
+
+    skip = z // hz != c
     holder = jnp.logical_not(skip)
-    send(buf["dw_fin"].at[sib], buf["dw_land"], id_dw_fin, dev_sib, skip)
-    router_last()
+    for kind in range(2):
+        value = reduce_last(True, kind, slice(0, HD), skip)
+
+        @pl.when(holder)
+        def _():
+            buf["dw_fin"][kind] = value()
+
+    send(buf["dw_fin"].at[sib], dw_land, id_dw_fin, dev_sib, skip)
+    keep(buf["dw_fin"].at[c], dw_land, holder)
 
     for j in range(2):
         for cc in range(2):
             own = jnp.logical_and(y == 2 * c + j, c == cc)
-            recv(buf["dq_land"].at[j, cc], id_dq + 2 * j + cc, own)
-        dq_ref[:, j * HD : (j + 1) * HD] = (
-            buf["dq_land"][j, 0].astype(F32) + buf["dq_land"][j, 1].astype(F32)
-        ).astype(BF)
-    for kind, ref in ((0, dk_ref), (1, dv_ref)):
+            recv(dq_land.at[j, cc], id_dq + 2 * j + cc, own)
+    for kind in range(2):
         for j in range(2):
             own = jnp.logical_and(y == 2 * c + j, half_y == c)
-            recv(buf["kv_land"].at[kind, j], id_kv_fin + 2 * kind + j, own)
-            ref[:, j * HD : (j + 1) * HD] = buf["kv_land"][kind, j]
-
-    recv(buf["dw_land"], id_dw_fin, holder)
-
-    @pl.when(holder)
-    def _():
-        dw_ref[...] = buf["dw_fin"][c]
-
-    @pl.when(skip)
-    def _():
-        dw_ref[...] = buf["dw_land"][...]
-
+            recv(kv_land.at[kind, j], id_kv_fin + 2 * kind + j, own)
+    recv(dw_land, id_dw_fin, holder)
+    for own, copy in local:
+        pl.when(own)(lambda: copy.wait())
     for unless, copy in sent:
         if unless is None:
             copy.wait_send()
         else:
             pl.when(jnp.logical_not(unless))(lambda: copy.wait_send())
 
-    lay.used = dict(counter)
-
-
-SEMS = 160
+
+SEMS = 220
+VMEM_LIMIT = 60 * 1024 * 1024
+
+
+def finish(dq_land, kv_land, dw_land, lg_in, dq_ref, dk_ref, dv_ref, dw_ref, lg_ref):
+    for j in range(2):
+        cols = slice(j * HD, (j + 1) * HD)
+        dq_ref[:, cols] = (dq_land[j, 0].astype(F32) + dq_land[j, 1].astype(F32)).astype(BF)
+        dk_ref[:, cols] = kv_land[0, j]
+        dv_ref[:, cols] = kv_land[1, j]
+    dw_ref[...] = dw_land[...]
+    lg_ref[...] = lg_in[...]
 
 
 def shards_fn(nz, nx):
@@ -665,28 +671,41 @@
         def kernel(*refs):
             fused(lay, names, *refs)
 
+        lands = pl.pallas_call(
+            kernel,
+            out_shape=(
+                jax.ShapeDtypeStruct((2, 2, HD, HD), BF),
+                jax.ShapeDtypeStruct((2, 2, HD, HD), BF),
+                jax.ShapeDtypeStruct((HD, 2 * HD), F32),
+                jax.ShapeDtypeStruct((1, HD), F32),
+            ),
+            in_specs=[any_, vmem, smem, smem, any_, any_, any_, any_],
+            out_specs=(any_, any_, any_, vmem),
+            scratch_shapes=list(scratch.values())
+            + [
+                pltpu.SemaphoreType.DMA((SEMS,)),
+                pltpu.SemaphoreType.DMA((SEMS,)),
+                pltpu.SemaphoreType.DMA((32,)),
+            ],
+            compiler_params=pltpu.CompilerParams(
+                collective_id=0, has_side_effects=True, vmem_limit_bytes=VMEM_LIMIT
+            ),
+            name="routed_backward",
+        )(grad, logit.reshape(1, -1), index, count, weight, q, k, v)
         out = pl.pallas_call(
-            kernel,
+            finish,
             out_shape=(
                 jax.ShapeDtypeStruct(q.shape, BF),
                 jax.ShapeDtypeStruct(q.shape, BF),
                 jax.ShapeDtypeStruct(q.shape, BF),
                 jax.ShapeDtypeStruct((HD, q.shape[1]), F32),
-                jax.ShapeDtypeStruct((1, logit.shape[0]), F32),
+                jax.ShapeDtypeStruct((1, HD), F32),
             ),
-            in_specs=[any_, vmem, smem, smem, any_, any_, any_, any_],
+            in_specs=[vmem] * 4,
             out_specs=(vmem,) * 5,
-            scratch_shapes=list(scratch.values())
-            + [
-                pltpu.SemaphoreType.DMA((SEMS,)),
-                pltpu.SemaphoreType.DMA((SEMS,)),
-                pltpu.SemaphoreType.DMA((16,)),
-            ],
-            compiler_params=pltpu.CompilerParams(
-                collective_id=0, has_side_effects=True, vmem_limit_bytes=48 * 1024 * 1024
-            ),
-            name="routed_backward",
-        )(grad, logit.reshape(1, -1), index, count, weight, q, k, v)
+            compiler_params=pltpu.CompilerParams(vmem_limit_bytes=VMEM_LIMIT),
+            name="finish",
+        )(*lands)
         return (*out[:4], out[4].reshape(-1))
 
     return run

time: 77.7 us -> 74.3 us (0.956)
  local copies, waits for them, and re-layouts: 10.4 us -> 0 us
  Pallas kernels: 66.4 us -> 73.5 us
    unnamed x21 -> x0, local copies, waits for them, and re-layouts: 10.4 us -> none
    pallas_call x1 -> x2, Pallas kernels: 66.4 us -> 73.5 us  [the longest x1 71.7 us: run(): pl.pallas_call(kernel, out_shape=(jax.ShapeDtypeStruct((2, 2, HD, HD), BF...]
where the time goes in v2:
time: 74.3 us; the launch traced here: 74.1 us
  Pallas kernels  73.5 us (99%)
    pallas_call x1, Pallas kernels, run(): pl.pallas_call(kernel, out_shape=(jax.ShapeDtypeStruct((2, 2, HD, HD), BF...  71.7 us
    pallas_call x1, Pallas kernels, run(): pl.pallas_call(finish, out_shape=(jax.ShapeDtypeStruct(q.shape, BF), jax....  1.77 us

profile of v2, /device:TPU:1, one launch (start us, length us, event | category | flops | bytes accessed | tf_op | source)
XLA Modules:
  0.0 74.1 jit_solution(18194627263078326690)
XLA Ops:
  0.6 71.7 %routed_backward.1 = (bf16[2,2,128,128]{3,2,1,0:T(8,128)(2,1)}, bf16[2,2,128,128]{3,2,1,0:T(8,128)(2,1)}, f32[128,256]{1,0:T(8,128)}, f32[1,128]{1,0:T(1,128)}) custom-call(bf16[128,4096]{1,0:T(8,128)(2,1)} %refs_0_.1, f32[1,128]{1,0:T(1,128)} %bitcast.2, s32[32]{0:T(128)} %refs_2_.1, s32[256]{0:T(256)} %refs_3_.1, bf16[256,4096]{1,0:T(8,128)(2,1)} %refs_4_.1, ...), custom_call_target="tpu_custom_call" | custom-call | tf_op jit(solution)/shard_map/routed_backward/pallas_call | solution.py:674
  72.4 1.8 %finish.1 = (bf16[128,256]{1,0:T(8,128)(2,1)}, bf16[128,256]{1,0:T(8,128)(2,1)}, bf16[128,256]{1,0:T(8,128)(2,1)}, f32[128,256]{1,0:T(8,128)}, f32[1,128]{1,0:T(1,128)}) custom-call(bf16[2,2,128,128]{3,2,1,0:T(8,128)(2,1)} %get-tuple-element.14.dq_land, bf16[2,2,128,128]{3,2,1,0:T(8,128)(2,1)} %get-tuple-element.15.kv_land, ...), custom_call_target="tpu_custom_call" | custom-call | tf_op jit(solution)/shard_map/finish/pallas_call | solution.py:695

commit v3 on v2

--- a/solution.py
+++ b/solution.py
@@ -55,11 +55,11 @@
             dqt=v((NY, HD, HD), F32),
             dkp=v((nz, 2 * HD, HD), F32),
             dvp=v((nz, 2 * HD, HD), F32),
-            dwp=v((2, hz, HD, 2 * HD), F32),
+            dwp=v((hz, HD, NY * HD), F32),
             kv_send=v((2, 2, steps, 2 * HD, HD), BF),
             kv_recv=v((2, 2, steps, 2 * HD, HD), BF),
-            dw_send=v((2, 2, steps, HD, 2 * HD), BF),
-            dw_recv=v((2, 2, steps, HD, 2 * HD), BF),
+            dw_send=v((2, steps, HD, NY * HD), BF),
+            dw_recv=v((2, steps, HD, NY * HD), BF),
             kv_fin=v((2, 2, HD, HD), BF),
             dq_out=v((NY, HD, HD), BF),
             dw_fin=v((2, HD, 2 * HD), F32),
@@ -97,22 +97,50 @@
         counter[kind] += n
         return first
 
-    sent = []
-
-    def send(src, dst, recv_id, to, unless=None):
+    ids = {}
+
+    def ident(*key):
+        if key not in ids:
+            ids[key] = alloc("recv")
+        return ids[key]
+
+    pool = [None] * POOL
+    singles = []
+
+    def wait_sent(entry):
+        unless, copy = entry
+        if unless is None:
+            copy.wait_send()
+        else:
+            pl.when(jnp.logical_not(unless))(lambda: copy.wait_send())
+
+    def send(src, dst, recv_id, to, unless=None, single=False):
+        if single:
+            slot = POOL + len(singles)
+        else:
+            slot = alloc("send") % POOL
+            if pool[slot] is not None:
+                wait_sent(pool[slot])
         copy = pltpu.make_async_remote_copy(
             src_ref=src,
             dst_ref=dst,
-            send_sem=send_sems.at[alloc("send")],
+            send_sem=send_sems.at[slot],
             recv_sem=recv_sems.at[recv_id],
             device_id=to,
             device_id_type=MESH,
         )
-        sent.append((unless, copy))
+        if single:
+            singles.append((unless, copy))
+        else:
+            pool[slot] = (unless, copy)
         if unless is None:
             copy.start()
         else:
             pl.when(jnp.logical_not(unless))(lambda: copy.start())
+
+    def keep(src, dst, recv_id, own):
+        copy = pltpu.make_async_copy(src, dst, recv_sems.at[recv_id])
+        pl.when(own)(lambda: copy.start())
 
     def recv(dst, recv_id, unless=None):
         copy = pltpu.make_async_remote_copy(
@@ -128,13 +156,6 @@
         else:
             pl.when(jnp.logical_not(unless))(lambda: copy.wait_recv())
 
-    local = []
-
-    def keep(src, dst, own):
-        copy = pltpu.make_async_copy(src, dst, local_sems.at[alloc("local")])
-        pl.when(own)(lambda: copy.start())
-        local.append((own, copy))
-
     grads_in = pltpu.make_async_copy(g_ref, buf["grads"], local_sems.at[alloc("local")])
     grads_in.start()
     own_half = pl.multiple_of(c * dh, HD)
@@ -157,33 +178,24 @@
     pl.semaphore_wait(barrier, len(partners))
 
     half_y = y // 2
-    id_k, id_v, id_q = alloc("recv", 2), alloc("recv", 2), alloc("recv", NY)
-    own_copies = []
+    id_k, id_v, id_q = alloc("recv"), alloc("recv"), alloc("recv")
+    for src, name, base in ((k_ref, "kk", id_k), (v_ref, "vv", id_v)):
+        for j in range(2):
+            y_to = 2 * c + j
+            own = jnp.logical_and(y_to == y, half_y == c)
+            part = pl.ds(pl.multiple_of((y % 2) * HD, HD), HD)
+            mine, dst = src.at[:, j * HD : (j + 1) * HD], buf[name].at[z, part, :]
+            send(mine, dst, base, dev(z, y_to, x, half_y), own)
+            keep(mine, dst, base, own)
     for j in range(2):
         y_to = 2 * c + j
-        own = jnp.logical_and(y_to == y, half_y == c)
-        cols = slice(j * HD, (j + 1) * HD)
-        part = pl.ds(pl.multiple_of((y % 2) * HD, HD), HD)
-        for src, name, base in ((k_ref, "kk", id_k), (v_ref, "vv", id_v)):
-            dst = buf[name].at[z, part, :]
-            send(src.at[:, cols], dst, base + y % 2, dev(z, y_to, x, half_y), own)
-            own_copies.append(
-                (own, pltpu.make_async_copy(src.at[:, cols], dst, local_sems.at[alloc("local")]))
-            )
-            pl.when(own)(lambda: own_copies[-1][1].start())
-    for j in range(2):
-        y_to = 2 * c + j
-        cols = slice(j * HD, (j + 1) * HD)
         for cc in range(2):
             own = jnp.logical_and(y_to == y, c == cc)
-            dst = buf["qh"].at[y]
-            send(q_ref.at[:, cols], dst, id_q + y, dev(z, y_to, x, cc), own)
-            own_copies.append(
-                (own, pltpu.make_async_copy(q_ref.at[:, cols], dst, local_sems.at[alloc("local")]))
-            )
-            pl.when(own)(lambda: own_copies[-1][1].start())
+            mine, dst = q_ref.at[:, j * HD : (j + 1) * HD], buf["qh"].at[y]
+            send(mine, dst, id_q, dev(z, y_to, x, cc), own)
+            keep(mine, dst, id_q, own)
     id_w = alloc("recv")
-    send(w_ref.at[:, pl.ds(other_half, dh)], buf["weight"].at[c], id_w, dev_sib)
+    send(w_ref.at[:, pl.ds(other_half, dh)], buf["weight"].at[c], id_w, dev_sib, single=True)
 
     slot = lax.broadcasted_iota(jnp.int32, (cap, HD), 0)
     lane = lax.broadcasted_iota(jnp.int32, (cap, HD), 1)
@@ -226,12 +238,13 @@
     id_rows_sib = alloc("recv")
     id_step_one = alloc("recv", 4)
     id_from_left, id_from_right = id_step_one, id_step_one + 2
-    id_far_left, id_far_right = alloc("recv"), alloc("recv")
-    send(buf["picked"].at[sib], row_slot(g), id_rows_sib, dev_sib)
+    id_far = alloc("recv")
+    send(buf["picked"].at[sib], row_slot(g), id_rows_sib, dev_sib, single=True)
     if nx > 1:
         for to, side in ((jnp.where(c == 0, right, left), c), (jnp.where(c == 0, left, right), sib)):
             for h in range(2):
-                send(buf["picked"].at[h], row_slot(g), id_step_one + 2 * side + c, dev(z, y, to, h))
+                dst, recv_id = row_slot(g), id_step_one + 2 * side + c
+                send(buf["picked"].at[h], dst, recv_id, dev(z, y, to, h), single=True)
     rows[pl.ds(pl.multiple_of(g * cap, cap), cap), :] = buf["picked"][c]
 
     buf["dkp"][...] = jnp.zeros_like(buf["dkp"])
@@ -242,13 +255,8 @@
     for i in range(NY):
         soft[i, HD : HD + 8, :] = jnp.full((8, HD), NEG, F32)
 
-    for j in range(2):
-        own = jnp.logical_and(c == half_y, y == 2 * c + j)
-        part = slice(j * HD, (j + 1) * HD)
-        recv(buf["kk"].at[z, part, :], id_k + j, own)
-        recv(buf["vv"].at[z, part, :], id_v + j, own)
-    for own, copy in own_copies:
-        pl.when(own)(lambda: copy.wait())
+    recv(buf["kk"].at[z], id_k)
+    recv(buf["vv"].at[z], id_v)
 
     halves = (slice(0, HD), slice(HD, 2 * HD))
     ring = [
@@ -256,18 +264,17 @@
         for name, n_up, n_down in (("kk", lay.far, lay.near), ("vv", lay.near, lay.far))
         for half in range(2)
     ]
-    id_ring = {(name, half): alloc("recv", 2 * (lay.far + 1)) for name, half, _, _ in ring}
 
     def ring_step(t):
         for name, half, n_up, n_down in ring:
-            base = id_ring[name, half]
             for side, hops in ((0, n_up), (1, n_down)):
                 b = (z + nz - t) % nz if side == 0 else (z + t) % nz
                 ref = buf[name].at[b, halves[half], :]
                 if 1 <= t <= hops:
-                    recv(ref, base + 2 * t + side)
+                    recv(ref, ident(name, half, t, side))
                 if t + 1 <= hops:
-                    send(ref, ref, base + 2 * (t + 1) + side, dev_up if side == 0 else dev_down)
+                    to = dev_up if side == 0 else dev_down
+                    send(ref, ref, ident(name, half, t + 1, side), to)
 
     ring_step(0)
 
@@ -296,30 +303,24 @@
         if t <= nz - 1 - t:
             pl.when(z + t >= nz)(lambda: forward_block((z + t) % nz, False))
 
-    for i in range(NY):
-        own = jnp.logical_and(c == half_y, y == i)
-        recv(buf["qh"].at[i], id_q + i, own)
-    forward_block(z, True)
-
     def rows_step_two():
         if nx == 1:
             return
         for cc in range(2):
             recv(row_slot(2 * left + cc), id_from_left + cc)
             recv(row_slot(2 * right + cc), id_from_right + cc)
-        send(row_slot(2 * left), row_slot(2 * left), id_far_left, dev(z, y, right, c))
-        send(row_slot(2 * right + 1), row_slot(2 * right + 1), id_far_right, dev(z, y, left, c))
-
-    id_slice, id_proj, id_go = alloc("recv", NY), alloc("recv"), alloc("recv", NY)
-    id_gate = alloc("recv", NY)
+        send(row_slot(2 * left), row_slot(2 * left), id_far, dev(z, y, right, c), single=True)
+        ref = row_slot(2 * right + 1)
+        send(ref, ref, id_far, dev(z, y, left, c), single=True)
+
+    id_slice, id_proj, id_go = alloc("recv"), alloc("recv"), alloc("recv")
+    id_gate = alloc("recv")
     row_iota = lax.broadcasted_iota(jnp.int32, (HD, shards * cap), 0)
 
     def project():
         recv(row_slot(2 * x + sib), id_rows_sib)
         if nx > 1:
-            opposite = (x + 2) % nx
-            recv(row_slot(2 * opposite), id_far_left)
-            recv(row_slot(2 * opposite + 1), id_far_right)
+            recv(rows.at[pl.ds(0, 2 * cap), :], id_far)
         lanes = lax.broadcasted_iota(jnp.int32, (1, shards * cap), 1)
         place = jnp.full((1, shards * cap), -1, jnp.int32)
         for i in range(shards):
@@ -337,7 +338,7 @@
         buf["gates"][y] = gate_rows[0:8, :]
         for dy in range(1, NY):
             y_to = (y + dy) % NY
-            send(buf["gates"].at[y], buf["gates"].at[y], id_gate + y, dev(z, y_to, x, c))
+            send(buf["gates"].at[y], buf["gates"].at[y], id_gate, dev(z, y_to, x, c))
         weight_in.wait()
         recv(buf["weight"].at[sib], id_w)
         part = buf["proj_part"]
@@ -355,11 +356,8 @@
             y_to = 2 * c + j
             for cc in range(2):
                 own = jnp.logical_and(y_to == y, c == cc)
-                send(buf["go_out"].at[j], buf["goh"].at[y], id_go + y, dev(z, y_to, x, cc), own)
-
-                @pl.when(own)
-                def _():
-                    buf["goh"][y] = buf["go_out"][j]
+                send(buf["go_out"].at[j], buf["goh"].at[y], id_go, dev(z, y_to, x, cc), own)
+                keep(buf["go_out"].at[j], buf["goh"].at[y], id_go, own)
 
         for dy in range(1, NY):
             y_to = (y + dy) % NY
@@ -367,29 +365,27 @@
             send(
                 buf["slice_out"].at[y_to],
                 buf["slices"].at[mine, :],
-                id_slice + y,
+                id_slice,
                 dev(z, y_to, x, c),
+                single=True,
             )
         buf["slices"][mine, :] = buf["slice_out"][y]
 
+    rows_step_two()
+    recv(buf["qh"], id_q)
+    forward_block(z, True)
     for t in range(1, lay.far + 1):
         ring_step(t)
         if t == 1:
-            rows_step_two()
+            project()
         if t == min(2, lay.far):
-            project()
-        if t == min(3, lay.far):
             out_gradient()
         forward_pair(t)
 
     id_soft = alloc("recv")
     send(soft, buf["soft_in"], id_soft, dev_sib)
-    for i in range(NY):
-        own = jnp.logical_and(c == half_y, y == i)
-        recv(buf["goh"].at[i], id_go + i, own)
-    for dy in range(1, NY):
-        yy = (y + dy) % NY
-        recv(buf["gates"].at[yy], id_gate + yy)
+    recv(buf["goh"], id_go)
+    recv(buf["gates"].at[pl.ds(0, NY - 1)], id_gate)
     recv(buf["soft_in"], id_soft)
     head_cols = pl.ds(pl.multiple_of(y * HD, HD), HD)
     soft_in = buf["soft_in"]
@@ -407,7 +403,7 @@
         buf["delta"][i, 0:1, :] = delta
         buf["router_out"][i] = jnp.broadcast_to(delta / gate_row, (8, HD))
 
-    id_outs, id_outs_sib, id_router_y = alloc("recv", NY), alloc("recv", NY), alloc("recv", NY)
+    id_outs, id_outs_sib, id_router_y = alloc("recv"), alloc("recv"), alloc("recv")
 
     def out_part(head, core):
         return buf["outs"].at[
@@ -418,8 +414,8 @@
     for dy in range(1, NY):
         y_to = (y + dy) % NY
         to = dev(z, y_to, x, c)
-        send(out_part(y, c), out_part(y, c), id_outs + y, to)
-        send(buf["router_out"].at[y_to], buf["router_y"].at[y], id_router_y + y, to)
+        send(out_part(y, c), out_part(y, c), id_outs, to)
+        send(buf["router_out"].at[y_to], buf["router_y"].at[y], id_router_y, to)
     buf["router_y"][y] = buf["router_out"][y]
 
     def backward_block(b, diagonal):
@@ -448,103 +444,80 @@
             pl.when(z + t >= nz)(lambda: backward_block((z + t) % nz, False))
 
     hops = ((lay.far, lay.near), (lay.near, lay.far))
-    id_kv = alloc("recv", 8 * (lay.far + 1))
-    id_dw = alloc("recv", 4 * (lay.far + 1))
 
     def target(direction, d):
         return (z + nz - d) % nz if direction == 0 else (z + d) % nz
 
-    def chain_id(dw, kind, direction, part):
-        steps = lay.far + 1
-        if dw:
-            return id_dw + (2 * kind + direction) * steps
-        return id_kv + (4 * (part.start // HD) + 2 * kind + direction) * steps
-
-    def reduce_step(d, dw):
+    dev_next = (dev_down, dev_up)
+
+    def kv_step(d, first):
+        inc = buf["kv_recv"]
         for kind in range(2):
-            for part in halves if not dw else (slice(0, HD),):
+            for part in halves:
                 for direction in range(2):
                     n = hops[kind][direction]
-                    if d > n:
+                    t = n - d
+                    if t < 0 or (t == 0) != first:
                         continue
-                    t = n - d
-                    b = target(direction, d)
-                    base = chain_id(dw, kind, direction, part)
-                    to = dev_down if direction == 0 else dev_up
-                    skip = b // hz != c if dw else None
-                    if dw:
-                        mine, out, inc = buf["dwp"].at[kind, b % hz], buf["dw_send"], buf["dw_recv"]
-                    else:
-                        mine = (buf["dkp"] if kind == 0 else buf["dvp"]).at[b, part, :]
-                        out, inc = buf["kv_send"], buf["kv_recv"]
-
-                    def value():
-                        total = mine[...]
-                        if t > 0:
-                            total = total + inc[kind, direction, t - 1, part, :].astype(F32)
-                        out[kind, direction, t, part, :] = total.astype(BF)
-
+                    key = ("chain", kind, direction, part.start)
+                    total = (buf["dkp"] if kind == 0 else buf["dvp"])[target(direction, d), part, :]
                     if t > 0:
-                        recv(inc.at[kind, direction, t - 1, part, :], base + t - 1, skip)
-                    if skip is None:
-                        value()
-                    else:
-                        pl.when(jnp.logical_not(skip))(value)
-                    send(
-                        out.at[kind, direction, t, part, :],
-                        inc.at[kind, direction, t, part, :],
-                        base + t,
-                        to,
-                        skip,
-                    )
-
-    def reduce_last(dw, kind, part, skip=None):
-        inc = buf["dw_recv"] if dw else buf["kv_recv"]
+                        recv(inc.at[kind, direction, t - 1, part, :], ident(*key, t - 1))
+                        total = total + inc[kind, direction, t - 1, part, :].astype(F32)
+                    out = buf["kv_send"].at[kind, direction, t, part, :]
+                    out[...] = total.astype(BF)
+                    to = dev_next[direction]
+                    send(out, inc.at[kind, direction, t, part, :], ident(*key, t), to)
+
+    def kv_last(kind, part):
+        inc = buf["kv_recv"]
+        total = (buf["dkp"] if kind == 0 else buf["dvp"])[z, part, :]
         for direction in range(2):
             n = hops[kind][direction]
             if n > 0:
-                base = chain_id(dw, kind, direction, part)
-                recv(inc.at[kind, direction, n - 1, part, :], base + n - 1, skip)
-
-        def value():
-            if dw:
-                total = buf["dwp"][kind, z % hz]
-            else:
-                total = (buf["dkp"] if kind == 0 else buf["dvp"])[z, part, :]
-            for direction in range(2):
-                n = hops[kind][direction]
-                if n > 0:
-                    total = total + inc[kind, direction, n - 1, part, :].astype(F32)
-            return total
-
-        return value
+                last = ident("chain", kind, direction, part.start, n - 1)
+                recv(inc.at[kind, direction, n - 1, part, :], last)
+                total = total + inc[kind, direction, n - 1, part, :].astype(F32)
+        return total
+
+    def dw_step(d):
+        inc = buf["dw_recv"]
+        for direction, n in enumerate(hops[0]):
+            t = n - d
+            if t < 0:
+                continue
+            b = target(direction, d)
+            skip = b // hz != c
+            out = buf["dw_send"].at[direction, t]
+            if t > 0:
+                recv(inc.at[direction, t - 1], ident("dw", direction, t - 1), skip)
+
+            @pl.when(jnp.logical_not(skip))
+            def _():
+                total = buf["dwp"][b % hz]
+                if t > 0:
+                    total = total + inc[direction, t - 1].astype(F32)
+                out[...] = total.astype(BF)
+
+            send(out, inc.at[direction, t], ident("dw", direction, t), dev_next[direction], skip)
 
     def share_outs():
+        recv(buf["outs"].at[: 2 * HD, : (NY - 1) * HD], id_outs)
         for dy in range(1, NY):
-            yy = (y + dy) % NY
-            recv(out_part(yy, c), id_outs + yy)
-            send(out_part(yy, c), out_part(yy, c), id_outs_sib + yy, dev_sib)
+            ref = out_part((y + dy) % NY, c)
+            send(ref, ref, id_outs_sib, dev_sib)
 
     def weight_gradient():
-        for dy in range(1, NY):
-            yy = (y + dy) % NY
-            recv(buf["slices"].at[pl.ds(pl.multiple_of(yy * HD, HD), HD), :], id_slice + yy)
-            recv(out_part(yy, sib), id_outs_sib + yy)
+        recv(buf["slices"].at[: (NY - 1) * HD, :], id_slice)
+        recv(buf["outs"].at[: 2 * HD, : (NY - 1) * HD], id_outs_sib)
         for i in range(hz):
-            for kind in range(2):
-                buf["dwp"][kind, i] = dot(
-                    buf["slices"][:, i * HD : (i + 1) * HD],
-                    buf["outs"][:, kind * 2 * HD : (kind + 1) * 2 * HD],
-                    0,
-                    0,
-                )
-
-    id_router_x = alloc("recv", nx)
+            part = buf["slices"][:, i * HD : (i + 1) * HD]
+            buf["dwp"][i] = dot(part, buf["outs"][...], 0, 0)
+
+    id_router_x = alloc("recv")
 
     def router_send():
-        for dy in range(1, NY):
-            yy = (y + dy) % NY
-            recv(buf["router_y"].at[yy], id_router_y + yy)
+        recv(buf["router_y"].at[: NY - 1], id_router_y)
         total = buf["router_y"][0]
         for i in range(1, NY):
             total = total + buf["router_y"][i]
@@ -552,12 +525,11 @@
         for dx in range(1, nx):
             x_to = (x + dx) % nx
             ref = buf["router_x"].at[x]
-            send(ref, ref, id_router_x + x, dev(z, y, x_to, c))
+            send(ref, ref, id_router_x, dev(z, y, x_to, c))
 
     def router_last():
-        for dx in range(1, nx):
-            xx = (x + dx) % nx
-            recv(buf["router_x"].at[xx], id_router_x + xx)
+        if nx > 1:
+            recv(buf["router_x"].at[: nx - 1], id_router_x)
         total = buf["router_x"][0]
         for i in range(1, nx):
             total = total + buf["router_x"][i]
@@ -569,83 +541,79 @@
         sig = 1.0 / (1.0 + jnp.exp(-logit_row))
         lg_ref[...] = placed[0:1, :] * sig * (1.0 - sig)
 
-    id_kv_fin, id_dq = alloc("recv", 4), alloc("recv", 4)
+    id_kv_fin, id_dq = alloc("recv"), alloc("recv")
     id_dw_fin = alloc("recv")
     side = y % 2
 
     def send_key_value_grads():
         for kind in range(2):
             for j in range(2):
-                final = reduce_last(False, kind, halves[j])()
+                final = kv_last(kind, halves[j])
                 if kind == 0:
                     final = final * factor
                 buf["kv_fin"][kind, j] = final.astype(BF)
                 y_to = 2 * c + j
                 own = jnp.logical_and(y_to == y, half_y == c)
                 src, dst = buf["kv_fin"].at[kind, j], kv_land.at[kind, side]
-                send(src, dst, id_kv_fin + 2 * kind + side, dev(z, y_to, x, half_y), own)
-                keep(src, dst, own)
+                send(src, dst, id_kv_fin, dev(z, y_to, x, half_y), own)
+                keep(src, dst, id_kv_fin, own)
 
     def send_query_grads():
         for i in range(NY):
             buf["dq_out"][i] = (buf["dqt"][i].T * factor).astype(BF)
             own = jnp.logical_and(y == i, half_y == c)
             src, dst = buf["dq_out"].at[i], dq_land.at[side, c]
-            send(src, dst, id_dq + 2 * side + c, dev(z, i, x, half_y), own)
-            keep(src, dst, own)
-
-    late = min(2, lay.far)
+            send(src, dst, id_dq, dev(z, i, x, half_y), own)
+            keep(src, dst, id_dq, own)
+
     for d in range(lay.far, 0, -1):
         backward_pair(d)
-        reduce_step(d, False)
-        if d == lay.far:
-            share_outs()
-        if d == late:
+        kv_step(d, True)
+    backward_block(z, True)
+    send_query_grads()
+    share_outs()
+    if lay.far == 1:
+        weight_gradient()
+        router_send()
+    for d in range(lay.far - 1, 0, -1):
+        kv_step(d, False)
+        if d == lay.far - 1:
             weight_gradient()
             router_send()
-            reduce_step(lay.far, True)
-        elif d < late:
-            reduce_step(lay.far - late + d, True)
-    backward_block(z, True)
-    send_query_grads()
-    for d in range(lay.far - late, 1, -1):
-        reduce_step(d, True)
+        dw_step(d + 1)
     send_key_value_grads()
-    if lay.far - late >= 1:
-        reduce_step(1, True)
+    dw_step(1)
     router_last()
 
     skip = z // hz != c
     holder = jnp.logical_not(skip)
-    for kind in range(2):
-        value = reduce_last(True, kind, slice(0, HD), skip)
-
-        @pl.when(holder)
-        def _():
-            buf["dw_fin"][kind] = value()
+    for direction, n in enumerate(hops[0]):
+        if n > 0:
+            recv(buf["dw_recv"].at[direction, n - 1], ident("dw", direction, n - 1), skip)
+
+    @pl.when(holder)
+    def _():
+        total = buf["dwp"][z % hz]
+        for direction, n in enumerate(hops[0]):
+            if n > 0:
+                total = total + buf["dw_recv"][direction, n - 1].astype(F32)
+        for core in range(2):
+            buf["dw_fin"][core] = total[:, core * 2 * HD : (core + 1) * 2 * HD]
 
     send(buf["dw_fin"].at[sib], dw_land, id_dw_fin, dev_sib, skip)
-    keep(buf["dw_fin"].at[c], dw_land, holder)
-
-    for j in range(2):
-        for cc in range(2):
-            own = jnp.logical_and(y == 2 * c + j, c == cc)
-            recv(dq_land.at[j, cc], id_dq + 2 * j + cc, own)
-    for kind in range(2):
-        for j in range(2):
-            own = jnp.logical_and(y == 2 * c + j, half_y == c)
-            recv(kv_land.at[kind, j], id_kv_fin + 2 * kind + j, own)
-    recv(dw_land, id_dw_fin, holder)
-    for own, copy in local:
-        pl.when(own)(lambda: copy.wait())
-    for unless, copy in sent:
-        if unless is None:
-            copy.wait_send()
-        else:
-            pl.when(jnp.logical_not(unless))(lambda: copy.wait_send())
-
-
-SEMS = 220
+    keep(buf["dw_fin"].at[c], dw_land, id_dw_fin, holder)
+
+    recv(dq_land, id_dq)
+    recv(kv_land, id_kv_fin)
+    recv(dw_land, id_dw_fin)
+    for entry in pool + singles:
+        if entry is not None:
+            wait_sent(entry)
+
+
+POOL = 24
+RECV_SEMS = 85
+SEND_SEMS = 35
 VMEM_LIMIT = 60 * 1024 * 1024
 
 
@@ -683,9 +651,9 @@
             out_specs=(any_, any_, any_, vmem),
             scratch_shapes=list(scratch.values())
             + [
-                pltpu.SemaphoreType.DMA((SEMS,)),
-                pltpu.SemaphoreType.DMA((SEMS,)),
-                pltpu.SemaphoreType.DMA((32,)),
+                pltpu.SemaphoreType.DMA((SEND_SEMS,)),
+                pltpu.SemaphoreType.DMA((RECV_SEMS,)),
+                pltpu.SemaphoreType.DMA((2,)),
             ],
             compiler_params=pltpu.CompilerParams(
                 collective_id=0, has_side_effects=True, vmem_limit_bytes=VMEM_LIMIT

time: 74.3 us -> 67 us (0.902)
  Pallas kernels: 73.5 us -> 66.3 us
    pallas_call x1, Pallas kernels: 71.7 us -> 64.5 us  [run(): pl.pallas_call(kernel, out_shape=(jax.ShapeDtypeStruct((2, 2, HD, HD), BF...]
where the time goes in v3:
time: 67 us; the launch traced here: 66.9 us
  Pallas kernels  66.3 us (99%)
    pallas_call x1, Pallas kernels, run(): pl.pallas_call(kernel, out_shape=(jax.ShapeDtypeStruct((2, 2, HD, HD), BF...  64.5 us
    pallas_call x1, Pallas kernels, run(): pl.pallas_call(finish, out_shape=(jax.ShapeDtypeStruct(q.shape, BF), jax....  1.77 us

profile of v3, /device:TPU:1, one launch (start us, length us, event | category | flops | bytes accessed | tf_op | source)
XLA Modules:
  0.0 66.9 jit_solution(917618352775572790)
XLA Ops:
  0.6 64.5 %routed_backward.1 = (bf16[2,2,128,128]{3,2,1,0:T(8,128)(2,1)}, bf16[2,2,128,128]{3,2,1,0:T(8,128)(2,1)}, f32[128,256]{1,0:T(8,128)}, f32[1,128]{1,0:T(1,128)}) custom-call(bf16[128,4096]{1,0:T(8,128)(2,1)} %refs_0_.1, f32[1,128]{1,0:T(1,128)} %bitcast.2, s32[32]{0:T(128)} %refs_2_.1, s32[256]{0:T(256)} %refs_3_.1, bf16[256,4096]{1,0:T(8,128)(2,1)} %refs_4_.1, ...), custom_call_target="tpu_custom_call" | custom-call | tf_op jit(solution)/shard_map/routed_backward/pallas_call | solution.py:642
  65.2 1.8 %finish.1 = (bf16[128,256]{1,0:T(8,128)(2,1)}, bf16[128,256]{1,0:T(8,128)(2,1)}, bf16[128,256]{1,0:T(8,128)(2,1)}, f32[128,256]{1,0:T(8,128)}, f32[1,128]{1,0:T(1,128)}) custom-call(bf16[2,2,128,128]{3,2,1,0:T(8,128)(2,1)} %get-tuple-element.14.dq_land, bf16[2,2,128,128]{3,2,1,0:T(8,128)(2,1)} %get-tuple-element.15.kv_land, ...), custom_call_target="tpu_custom_call" | custom-call | tf_op jit(solution)/shard_map/finish/pallas_call | solution.py:663

commit v4 on v3

--- a/solution.py
+++ b/solution.py
@@ -58,8 +58,8 @@
             dwp=v((hz, HD, NY * HD), F32),
             kv_send=v((2, 2, steps, 2 * HD, HD), BF),
             kv_recv=v((2, 2, steps, 2 * HD, HD), BF),
-            dw_send=v((2, steps, HD, NY * HD), BF),
-            dw_recv=v((2, steps, HD, NY * HD), BF),
+            dw_send=v((2, 2, steps, HD, 2 * HD), BF),
+            dw_recv=v((2, 2, steps, HD, 2 * HD), BF),
             kv_fin=v((2, 2, HD, HD), BF),
             dq_out=v((NY, HD, HD), BF),
             dw_fin=v((2, HD, 2 * HD), F32),
@@ -376,9 +376,8 @@
     forward_block(z, True)
     for t in range(1, lay.far + 1):
         ring_step(t)
-        if t == 1:
+        if t == min(2, lay.far):
             project()
-        if t == min(2, lay.far):
             out_gradient()
         forward_pair(t)
 
@@ -450,17 +449,17 @@
 
     dev_next = (dev_down, dev_up)
 
-    def kv_step(d, first):
+    def kv_step(t):
         inc = buf["kv_recv"]
         for kind in range(2):
             for part in halves:
                 for direction in range(2):
                     n = hops[kind][direction]
-                    t = n - d
-                    if t < 0 or (t == 0) != first:
+                    if t >= n:
                         continue
                     key = ("chain", kind, direction, part.start)
-                    total = (buf["dkp"] if kind == 0 else buf["dvp"])[target(direction, d), part, :]
+                    b = target(direction, n - t)
+                    total = (buf["dkp"] if kind == 0 else buf["dvp"])[b, part, :]
                     if t > 0:
                         recv(inc.at[kind, direction, t - 1, part, :], ident(*key, t - 1))
                         total = total + inc[kind, direction, t - 1, part, :].astype(F32)
@@ -480,26 +479,28 @@
                 total = total + inc[kind, direction, n - 1, part, :].astype(F32)
         return total
 
-    def dw_step(d):
+    def dw_step(t):
         inc = buf["dw_recv"]
-        for direction, n in enumerate(hops[0]):
-            t = n - d
-            if t < 0:
-                continue
-            b = target(direction, d)
-            skip = b // hz != c
-            out = buf["dw_send"].at[direction, t]
-            if t > 0:
-                recv(inc.at[direction, t - 1], ident("dw", direction, t - 1), skip)
-
-            @pl.when(jnp.logical_not(skip))
-            def _():
-                total = buf["dwp"][b % hz]
+        for half in range(2):
+            for direction in range(2):
+                n = hops[half][direction]
+                if t >= n:
+                    continue
+                b = target(direction, n - t)
+                skip = b // hz != c
+                out = buf["dw_send"].at[half, direction, t]
                 if t > 0:
-                    total = total + inc[direction, t - 1].astype(F32)
-                out[...] = total.astype(BF)
-
-            send(out, inc.at[direction, t], ident("dw", direction, t), dev_next[direction], skip)
+                    recv(inc.at[half, direction, t - 1], ident("dw", half, direction, t - 1), skip)
+
+                @pl.when(jnp.logical_not(skip))
+                def _():
+                    total = buf["dwp"][b % hz, :, half * 2 * HD : (half + 1) * 2 * HD]
+                    if t > 0:
+                        total = total + inc[half, direction, t - 1].astype(F32)
+                    out[...] = total.astype(BF)
+
+                to = dev_next[direction]
+                send(out, inc.at[half, direction, t], ident("dw", half, direction, t), to, skip)
 
     def share_outs():
         recv(buf["outs"].at[: 2 * HD, : (NY - 1) * HD], id_outs)
@@ -568,37 +569,42 @@
 
     for d in range(lay.far, 0, -1):
         backward_pair(d)
-        kv_step(d, True)
+        if d == max(lay.near, 1):
+            kv_step(0)
     backward_block(z, True)
     send_query_grads()
+    if lay.far > 1:
+        kv_step(1)
     share_outs()
-    if lay.far == 1:
-        weight_gradient()
-        router_send()
-    for d in range(lay.far - 1, 0, -1):
-        kv_step(d, False)
-        if d == lay.far - 1:
-            weight_gradient()
-            router_send()
-        dw_step(d + 1)
+    router_send()
+    weight_gradient()
+    dw_step(0)
+    for t in range(2, lay.far):
+        kv_step(t)
+        dw_step(t - 1)
     send_key_value_grads()
-    dw_step(1)
     router_last()
+    if lay.far > 1:
+        dw_step(lay.far - 1)
 
     skip = z // hz != c
     holder = jnp.logical_not(skip)
-    for direction, n in enumerate(hops[0]):
-        if n > 0:
-            recv(buf["dw_recv"].at[direction, n - 1], ident("dw", direction, n - 1), skip)
+    for half in range(2):
+        for direction in range(2):
+            n = hops[half][direction]
+            if n > 0:
+                key = ident("dw", half, direction, n - 1)
+                recv(buf["dw_recv"].at[half, direction, n - 1], key, skip)
 
     @pl.when(holder)
     def _():
-        total = buf["dwp"][z % hz]
-        for direction, n in enumerate(hops[0]):
-            if n > 0:
-                total = total + buf["dw_recv"][direction, n - 1].astype(F32)
-        for core in range(2):
-            buf["dw_fin"][core] = total[:, core * 2 * HD : (core + 1) * 2 * HD]
+        for half in range(2):
+            total = buf["dwp"][z % hz, :, half * 2 * HD : (half + 1) * 2 * HD]
+            for direction in range(2):
+                n = hops[half][direction]
+                if n > 0:
+                    total = total + buf["dw_recv"][half, direction, n - 1].astype(F32)
+            buf["dw_fin"][half] = total
 
     send(buf["dw_fin"].at[sib], dw_land, id_dw_fin, dev_sib, skip)
     keep(buf["dw_fin"].at[c], dw_land, id_dw_fin, holder)
@@ -612,7 +618,7 @@
 
 
 POOL = 24
-RECV_SEMS = 85
+RECV_SEMS = 92
 SEND_SEMS = 35
 VMEM_LIMIT = 60 * 1024 * 1024
 

time: 67 us -> 63.5 us (0.948)
  Pallas kernels: 66.3 us -> 62.7 us
    pallas_call x1, Pallas kernels: 64.5 us -> 61 us  [run(): pl.pallas_call(kernel, out_shape=(jax.ShapeDtypeStruct((2, 2, HD, HD), BF...]
where the time goes in v4:
time: 63.5 us; the launch traced here: 63.4 us
  Pallas kernels  62.7 us (99%)
  between operations  0.64 us (1%)
    pallas_call x1, Pallas kernels, run(): pl.pallas_call(kernel, out_shape=(jax.ShapeDtypeStruct((2, 2, HD, HD), BF...  61 us
    pallas_call x1, Pallas kernels, run(): pl.pallas_call(finish, out_shape=(jax.ShapeDtypeStruct(q.shape, BF), jax....  1.77 us

profile of v4, /device:TPU:1, one launch (start us, length us, event | category | flops | bytes accessed | tf_op | source)
XLA Modules:
  0.0 63.4 jit_solution(18362711248862684453)
XLA Ops:
  0.6 61.0 %routed_backward.1 = (bf16[2,2,128,128]{3,2,1,0:T(8,128)(2,1)}, bf16[2,2,128,128]{3,2,1,0:T(8,128)(2,1)}, f32[128,256]{1,0:T(8,128)}, f32[1,128]{1,0:T(1,128)}) custom-call(bf16[128,4096]{1,0:T(8,128)(2,1)} %refs_0_.1, f32[1,128]{1,0:T(1,128)} %bitcast.2, s32[32]{0:T(128)} %refs_2_.1, s32[256]{0:T(256)} %refs_3_.1, bf16[256,4096]{1,0:T(8,128)(2,1)} %refs_4_.1, ...), custom_call_target="tpu_custom_call" | custom-call | tf_op jit(solution)/shard_map/routed_backward/pallas_call | solution.py:648
  61.6 1.8 %finish.1 = (bf16[128,256]{1,0:T(8,128)(2,1)}, bf16[128,256]{1,0:T(8,128)(2,1)}, bf16[128,256]{1,0:T(8,128)(2,1)}, f32[128,256]{1,0:T(8,128)}, f32[1,128]{1,0:T(1,128)}) custom-call(bf16[2,2,128,128]{3,2,1,0:T(8,128)(2,1)} %get-tuple-element.14.dq_land, bf16[2,2,128,128]{3,2,1,0:T(8,128)(2,1)} %get-tuple-element.15.kv_land, ...), custom_call_target="tpu_custom_call" | custom-call | tf_op jit(solution)/shard_map/finish/pallas_call | solution.py:669

commit v5 on v4

--- a/solution.py
+++ b/solution.py
@@ -11,6 +11,7 @@
 BF = jnp.bfloat16
 F32 = jnp.float32
 NEG = -1e30
+LOG2E = 1.4426950408889634
 
 
 def dot(a, b, ca, cb, precision=None):
@@ -43,26 +44,27 @@
             proj_part=v((2, HD, 2 * HD), F32),
             proj_in=v((HD, 2 * HD), F32),
             go_out=v((2, HD, HD), BF),
-            qh=v((NY, HD, HD), BF),
-            goh=v((NY, HD, HD), BF),
+            qh=v((NY * HD, HD), BF),
+            goh=v((NY * HD, HD), BF),
             kk=v((nz, 2 * HD, HD), BF),
             vv=v((nz, 2 * HD, HD), BF),
-            soft=v((NY, HD + 16, HD), F32),
-            soft_in=v((NY, HD + 16, HD), F32),
-            lse=v((NY, 8, HD), F32),
-            delta=v((NY, 8, HD), F32),
+            soft=v((HD + 16, NY * HD), F32),
+            soft_in=v((HD + 16, NY * HD), F32),
+            lse=v((8, NY * HD), F32),
+            delta=v((8, NY * HD), F32),
             outs=v((NY * HD, NY * HD), BF),
-            dqt=v((NY, HD, HD), F32),
+            dqt=v((HD, NY * HD), F32),
             dkp=v((nz, 2 * HD, HD), F32),
             dvp=v((nz, 2 * HD, HD), F32),
-            dwp=v((hz, HD, NY * HD), F32),
+            dw_mine=v((2, HD, 2 * HD), F32),
+            dw_own=v((HD, 2 * HD), F32),
             kv_send=v((2, 2, steps, 2 * HD, HD), BF),
             kv_recv=v((2, 2, steps, 2 * HD, HD), BF),
             dw_send=v((2, 2, steps, HD, 2 * HD), BF),
             dw_recv=v((2, 2, steps, HD, 2 * HD), BF),
             kv_fin=v((2, 2, HD, HD), BF),
             dq_out=v((NY, HD, HD), BF),
-            dw_fin=v((2, HD, 2 * HD), F32),
+            dw_fin=v((HD, 2 * HD), F32),
             router_out=v((NY, 8, HD), F32),
             router_y=v((NY, 8, HD), F32),
             router_x=v((nx, 8, HD), F32),
@@ -89,6 +91,7 @@
     up, down = (z + 1) % nz, (z + nz - 1) % nz
     dev_up, dev_down = dev(up, y, x, c), dev(down, y, x, c)
     dev_sib = dev(z, y, x, sib)
+    my_rows = pl.ds(pl.multiple_of(y * HD, HD), HD)
 
     counter = {"send": 0, "recv": 0, "local": 0}
 
@@ -191,7 +194,7 @@
         y_to = 2 * c + j
         for cc in range(2):
             own = jnp.logical_and(y_to == y, c == cc)
-            mine, dst = q_ref.at[:, j * HD : (j + 1) * HD], buf["qh"].at[y]
+            mine, dst = q_ref.at[:, j * HD : (j + 1) * HD], buf["qh"].at[my_rows, :]
             send(mine, dst, id_q, dev(z, y_to, x, cc), own)
             keep(mine, dst, id_q, own)
     id_w = alloc("recv")
@@ -252,11 +255,7 @@
     buf["dqt"][...] = jnp.zeros_like(buf["dqt"])
     soft = buf["soft"]
     soft[...] = jnp.zeros_like(soft)
-    for i in range(NY):
-        soft[i, HD : HD + 8, :] = jnp.full((8, HD), NEG, F32)
-
-    recv(buf["kk"].at[z], id_k)
-    recv(buf["vv"].at[z], id_v)
+    soft[HD : HD + 8, :] = jnp.full((8, NY * HD), NEG, F32)
 
     halves = (slice(0, HD), slice(HD, 2 * HD))
     ring = [
@@ -267,6 +266,8 @@
 
     def ring_step(t):
         for name, half, n_up, n_down in ring:
+            if t == 0 and half == 0:
+                recv(buf[name].at[z], id_k if name == "kk" else id_v)
             for side, hops in ((0, n_up), (1, n_down)):
                 b = (z + nz - t) % nz if side == 0 else (z + t) % nz
                 ref = buf[name].at[b, halves[half], :]
@@ -278,25 +279,26 @@
 
     ring_step(0)
 
-    def allowed(i):
-        key = c * 2 * HD + lax.broadcasted_iota(jnp.int32, (2 * HD, HD), 0)
-        query = i * HD + lax.broadcasted_iota(jnp.int32, (2 * HD, HD), 1)
+    def allowed():
+        key = c * 2 * HD + lax.broadcasted_iota(jnp.int32, (2 * HD, NY * HD), 0)
+        query = lax.broadcasted_iota(jnp.int32, (2 * HD, NY * HD), 1)
         return key <= query
+
+    factor2 = factor * LOG2E
 
     def forward_block(b, diagonal):
         keys, values = buf["kk"][b], buf["vv"][b]
-        for i in range(NY):
-            scores = dot(keys, buf["qh"][i], 1, 1) * factor
-            if diagonal:
-                scores = jnp.where(allowed(i), scores, NEG)
-            old = soft[i, HD : HD + 1, :]
-            new = jnp.maximum(old, jnp.max(scores, axis=0, keepdims=True))
-            weights = jnp.exp(scores - new)
-            decay = jnp.exp(old - new)
-            norm = soft[i, HD + 8 : HD + 9, :] * decay + jnp.sum(weights, axis=0, keepdims=True)
-            soft[i, 0:HD, :] = soft[i, 0:HD, :] * decay + dot(values, weights.astype(BF), 0, 0)
-            soft[i, HD : HD + 1, :] = new
-            soft[i, HD + 8 : HD + 9, :] = norm
+        scores = dot(keys, buf["qh"][...], 1, 1) * factor2
+        if diagonal:
+            scores = jnp.where(allowed(), scores, NEG)
+        old = soft[HD : HD + 1, :]
+        new = jnp.maximum(old, jnp.max(scores, axis=0, keepdims=True))
+        weights = jnp.exp2(scores - new)
+        decay = jnp.exp2(old - new)
+        norm = soft[HD + 8 : HD + 9, :] * decay + jnp.sum(weights, axis=0, keepdims=True)
+        soft[0:HD, :] = soft[0:HD, :] * decay + dot(values, weights.astype(BF), 0, 0)
+        soft[HD : HD + 1, :] = new
+        soft[HD + 8 : HD + 9, :] = norm
 
     def forward_pair(t):
         pl.when(z >= t)(lambda: forward_block((z + nz - t) % nz, False))
@@ -356,20 +358,19 @@
             y_to = 2 * c + j
             for cc in range(2):
                 own = jnp.logical_and(y_to == y, c == cc)
-                send(buf["go_out"].at[j], buf["goh"].at[y], id_go, dev(z, y_to, x, cc), own)
-                keep(buf["go_out"].at[j], buf["goh"].at[y], id_go, own)
+                send(buf["go_out"].at[j], buf["goh"].at[my_rows, :], id_go, dev(z, y_to, x, cc), own)
+                keep(buf["go_out"].at[j], buf["goh"].at[my_rows, :], id_go, own)
 
         for dy in range(1, NY):
             y_to = (y + dy) % NY
-            mine = pl.ds(pl.multiple_of(y * HD, HD), HD)
             send(
                 buf["slice_out"].at[y_to],
-                buf["slices"].at[mine, :],
+                buf["slices"].at[my_rows, :],
                 id_slice,
                 dev(z, y_to, x, c),
                 single=True,
             )
-        buf["slices"][mine, :] = buf["slice_out"][y]
+        buf["slices"][my_rows, :] = buf["slice_out"][y]
 
     rows_step_two()
     recv(buf["qh"], id_q)
@@ -388,18 +389,20 @@
     recv(buf["soft_in"], id_soft)
     head_cols = pl.ds(pl.multiple_of(y * HD, HD), HD)
     soft_in = buf["soft_in"]
+    max_a, max_b = soft[HD : HD + 1, :], soft_in[HD : HD + 1, :]
+    top = jnp.maximum(max_a, max_b)
+    scale_a, scale_b = jnp.exp2(max_a - top), jnp.exp2(max_b - top)
+    norm = soft[HD + 8 : HD + 9, :] * scale_a + soft_in[HD + 8 : HD + 9, :] * scale_b
+    buf["lse"][0:1, :] = top + jnp.log2(norm)
+    scale_a, scale_b = scale_a / norm, scale_b / norm
     for i in range(NY):
-        max_a, max_b = soft[i, HD : HD + 1, :], soft_in[i, HD : HD + 1, :]
-        top = jnp.maximum(max_a, max_b)
-        scale_a, scale_b = jnp.exp(max_a - top), jnp.exp(max_b - top)
-        norm = soft[i, HD + 8 : HD + 9, :] * scale_a + soft_in[i, HD + 8 : HD + 9, :] * scale_b
-        out_t = (soft[i, 0:HD, :] * scale_a + soft_in[i, 0:HD, :] * scale_b) / norm
+        span = slice(i * HD, (i + 1) * HD)
+        out_t = soft[0:HD, span] * scale_a[:, span] + soft_in[0:HD, span] * scale_b[:, span]
         out_t = out_t.astype(BF).astype(F32)
         gate_row = buf["gates"][i, 0:1, :]
-        buf["outs"][i * HD : (i + 1) * HD, head_cols] = (gate_row * out_t).T.astype(BF)
-        buf["lse"][i, 0:1, :] = top + jnp.log(norm)
-        delta = jnp.sum(out_t * buf["goh"][i].astype(F32).T, axis=0, keepdims=True)
-        buf["delta"][i, 0:1, :] = delta
+        buf["outs"][span, head_cols] = (gate_row * out_t).T.astype(BF)
+        delta = jnp.sum(out_t * buf["goh"][span, :].astype(F32).T, axis=0, keepdims=True)
+        buf["delta"][0:1, span] = delta
         buf["router_out"][i] = jnp.broadcast_to(delta / gate_row, (8, HD))
 
     id_outs, id_outs_sib, id_router_y = alloc("recv"), alloc("recv"), alloc("recv")
@@ -419,23 +422,16 @@
 
     def backward_block(b, diagonal):
         keys, values = buf["kk"][b], buf["vv"][b]
-        for i in range(NY):
-            queries, go = buf["qh"][i], buf["goh"][i]
-            scores = dot(keys, queries, 1, 1) * factor
-            weights = jnp.exp(scores - buf["lse"][i, 0:1, :])
-            if diagonal:
-                weights = jnp.where(allowed(i), weights, 0.0)
-            grad_weights = dot(values, go, 1, 1)
-            grad_scores = (weights * (grad_weights - buf["delta"][i, 0:1, :])).astype(BF)
-            value_part = dot(weights.astype(BF), go, 1, 0)
-            key_part = dot(grad_scores, queries, 1, 0)
-            if i == 0:
-                buf["dvp"][b] = value_part
-                buf["dkp"][b] = key_part
-            else:
-                buf["dvp"][b] += value_part
-                buf["dkp"][b] += key_part
-            buf["dqt"][i] += dot(keys, grad_scores, 0, 0)
+        queries, go = buf["qh"][...], buf["goh"][...]
+        scores = dot(keys, queries, 1, 1) * factor2
+        weights = jnp.exp2(scores - buf["lse"][0:1, :])
+        if diagonal:
+            weights = jnp.where(allowed(), weights, 0.0)
+        grad_weights = dot(values, go, 1, 1)
+        grad_scores = (weights * (grad_weights - buf["delta"][0:1, :])).astype(BF)
+        buf["dvp"][b] = dot(weights.astype(BF), go, 1, 0)
+        buf["dkp"][b] = dot(grad_scores, queries, 1, 0)
+        buf["dqt"][...] += dot(keys, grad_scores, 0, 0)
 
     def backward_pair(t):
         pl.when(z >= t)(lambda: backward_block((z + nz - t) % nz, False))
@@ -479,6 +475,10 @@
                 total = total + inc[kind, direction, n - 1, part, :].astype(F32)
         return total
 
+    def dw_part(b, half):
+        rows_of = buf["slices"][:, pl.ds(pl.multiple_of((b % hz) * HD, HD), HD)]
+        return dot(rows_of, buf["outs"][:, half * 2 * HD : (half + 1) * 2 * HD], 0, 0)
+
     def dw_step(t):
         inc = buf["dw_recv"]
         for half in range(2):
@@ -494,13 +494,45 @@
 
                 @pl.when(jnp.logical_not(skip))
                 def _():
-                    total = buf["dwp"][b % hz, :, half * 2 * HD : (half + 1) * 2 * HD]
+                    total = dw_part(b, half)
                     if t > 0:
                         total = total + inc[half, direction, t - 1].astype(F32)
                     out[...] = total.astype(BF)
 
                 to = dev_next[direction]
+                if t == n - 1:
+                    to = dev(down if direction == 0 else up, y, x, half)
                 send(out, inc.at[half, direction, t], ident("dw", half, direction, t), to, skip)
+
+    id_dw_own = alloc("recv")
+    not_holder = z // hz != c
+    holder = jnp.logical_not(not_holder)
+
+    def dw_own_block():
+        @pl.when(holder)
+        def _():
+            for half in range(2):
+                buf["dw_mine"][half] = dw_part(z, half)
+            buf["dw_own"][...] = buf["dw_mine"][c]
+
+        send(buf["dw_mine"].at[sib], buf["dw_own"], id_dw_own, dev_sib, not_holder)
+
+    def dw_last():
+        recv(buf["dw_own"], id_dw_own, holder)
+        for half in range(2):
+
+            @pl.when(c == half)
+            def _():
+                total = buf["dw_own"][...]
+                for direction in range(2):
+                    n = hops[half][direction]
+                    if n > 0:
+                        recv(
+                            buf["dw_recv"].at[half, direction, n - 1],
+                            ident("dw", half, direction, n - 1),
+                        )
+                        total = total + buf["dw_recv"][half, direction, n - 1].astype(F32)
+                buf["dw_fin"][...] = total
 
     def share_outs():
         recv(buf["outs"].at[: 2 * HD, : (NY - 1) * HD], id_outs)
@@ -508,12 +540,9 @@
             ref = out_part((y + dy) % NY, c)
             send(ref, ref, id_outs_sib, dev_sib)
 
-    def weight_gradient():
+    def take_outs():
         recv(buf["slices"].at[: (NY - 1) * HD, :], id_slice)
         recv(buf["outs"].at[: 2 * HD, : (NY - 1) * HD], id_outs_sib)
-        for i in range(hz):
-            part = buf["slices"][:, i * HD : (i + 1) * HD]
-            buf["dwp"][i] = dot(part, buf["outs"][...], 0, 0)
 
     id_router_x = alloc("recv")
 
@@ -543,7 +572,6 @@
         lg_ref[...] = placed[0:1, :] * sig * (1.0 - sig)
 
     id_kv_fin, id_dq = alloc("recv"), alloc("recv")
-    id_dw_fin = alloc("recv")
     side = y % 2
 
     def send_key_value_grads():
@@ -561,7 +589,7 @@
 
     def send_query_grads():
         for i in range(NY):
-            buf["dq_out"][i] = (buf["dqt"][i].T * factor).astype(BF)
+            buf["dq_out"][i] = (buf["dqt"][:, i * HD : (i + 1) * HD].T * factor).astype(BF)
             own = jnp.logical_and(y == i, half_y == c)
             src, dst = buf["dq_out"].at[i], dq_land.at[side, c]
             send(src, dst, id_dq, dev(z, i, x, half_y), own)
@@ -577,41 +605,24 @@
         kv_step(1)
     share_outs()
     router_send()
-    weight_gradient()
+    take_outs()
     dw_step(0)
     for t in range(2, lay.far):
         kv_step(t)
         dw_step(t - 1)
     send_key_value_grads()
+    dw_own_block()
     router_last()
     if lay.far > 1:
         dw_step(lay.far - 1)
 
-    skip = z // hz != c
-    holder = jnp.logical_not(skip)
-    for half in range(2):
-        for direction in range(2):
-            n = hops[half][direction]
-            if n > 0:
-                key = ident("dw", half, direction, n - 1)
-                recv(buf["dw_recv"].at[half, direction, n - 1], key, skip)
-
-    @pl.when(holder)
-    def _():
-        for half in range(2):
-            total = buf["dwp"][z % hz, :, half * 2 * HD : (half + 1) * 2 * HD]
-            for direction in range(2):
-                n = hops[half][direction]
-                if n > 0:
-                    total = total + buf["dw_recv"][half, direction, n - 1].astype(F32)
-            buf["dw_fin"][half] = total
-
-    send(buf["dw_fin"].at[sib], dw_land, id_dw_fin, dev_sib, skip)
-    keep(buf["dw_fin"].at[c], dw_land, id_dw_fin, holder)
+    dw_last()
+    dw_out = pltpu.make_async_copy(buf["dw_fin"], dw_land, local_sems.at[alloc("local")])
+    dw_out.start()
 
     recv(dq_land, id_dq)
     recv(kv_land, id_kv_fin)
-    recv(dw_land, id_dw_fin)
+    dw_out.wait()
     for entry in pool + singles:
         if entry is not None:
             wait_sent(entry)
@@ -659,7 +670,7 @@
             + [
                 pltpu.SemaphoreType.DMA((SEND_SEMS,)),
                 pltpu.SemaphoreType.DMA((RECV_SEMS,)),
-                pltpu.SemaphoreType.DMA((2,)),
+                pltpu.SemaphoreType.DMA((3,)),
             ],
             compiler_params=pltpu.CompilerParams(
                 collective_id=0, has_side_effects=True, vmem_limit_bytes=VMEM_LIMIT

time: 63.5 us -> 60.1 us (0.946)
  Pallas kernels: 62.7 us -> 59.4 us
    pallas_call x1, Pallas kernels: 61 us -> 57.6 us  [run(): pl.pallas_call(kernel, out_shape=(jax.ShapeDtypeStruct((2, 2, HD, HD), BF...]
where the time goes in v5:
time: 60.1 us; the launch traced here: 60 us
  Pallas kernels  59.4 us (99%)
  between operations  0.64 us (1%)
    pallas_call x1, Pallas kernels, run(): pl.pallas_call(kernel, out_shape=(jax.ShapeDtypeStruct((2, 2, HD, HD), BF...  57.6 us
    pallas_call x1, Pallas kernels, run(): pl.pallas_call(finish, out_shape=(jax.ShapeDtypeStruct(q.shape, BF), jax....  1.77 us

profile of v5, /device:TPU:1, one launch (start us, length us, event | category | flops | bytes accessed | tf_op | source)
XLA Modules:
  0.0 60.0 jit_solution(12925695622094194630)
XLA Ops:
  0.6 57.6 %routed_backward.1 = (bf16[2,2,128,128]{3,2,1,0:T(8,128)(2,1)}, bf16[2,2,128,128]{3,2,1,0:T(8,128)(2,1)}, f32[128,256]{1,0:T(8,128)}, f32[1,128]{1,0:T(1,128)}) custom-call(bf16[128,4096]{1,0:T(8,128)(2,1)} %refs_0_.1, f32[1,128]{1,0:T(1,128)} %bitcast.2, s32[32]{0:T(128)} %refs_2_.1, s32[256]{0:T(256)} %refs_3_.1, bf16[256,4096]{1,0:T(8,128)(2,1)} %refs_4_.1, ...), custom_call_target="tpu_custom_call" | custom-call | tf_op jit(solution)/shard_map/routed_backward/pallas_call | solution.py:659
  58.2 1.8 %finish.1 = (bf16[128,256]{1,0:T(8,128)(2,1)}, bf16[128,256]{1,0:T(8,128)(2,1)}, bf16[128,256]{1,0:T(8,128)(2,1)}, f32[128,256]{1,0:T(8,128)}, f32[1,128]{1,0:T(1,128)}) custom-call(bf16[2,2,128,128]{3,2,1,0:T(8,128)(2,1)} %get-tuple-element.14.dq_land, bf16[2,2,128,128]{3,2,1,0:T(8,128)(2,1)} %get-tuple-element.15.kv_land, ...), custom_call_target="tpu_custom_call" | custom-call | tf_op jit(solution)/shard_map/finish/pallas_call | solution.py:680

commit v6 on v5

--- a/solution.py
+++ b/solution.py
@@ -1,3 +1,5 @@
+import functools
+
 import jax
 import jax.numpy as jnp
 from jax import lax
@@ -11,6 +13,7 @@
 BF = jnp.bfloat16
 F32 = jnp.float32
 NEG = -1e30
+FAR_WAY = dict(kk=1, vv=0)
 LOG2E = 1.4426950408889634
 
 
@@ -27,6 +30,14 @@
         self.hz = nz // 2
         self.far = nz // 2
         self.near = nz - 1 - self.far
+        self.relay = max(self.near - 1, 0)
+
+    def needed(self, b, wrapped, d, is_far):
+        if not wrapped:
+            return b + d <= self.nz - 1
+        if d == self.far:
+            return b <= self.far - 1
+        return b <= (self.far if is_far and d <= self.relay else self.near) - 1
 
     def scratch(self):
         nz, nx, cap, d, dh, hz = self.nz, self.nx, self.cap, self.d, self.dh, self.hz
@@ -91,7 +102,12 @@
     up, down = (z + 1) % nz, (z + nz - 1) % nz
     dev_up, dev_down = dev(up, y, x, c), dev(down, y, x, c)
     dev_sib = dev(z, y, x, sib)
+    near, far, relay = lay.near, lay.far, lay.relay
+    jump = far - relay
+    z_jump = ((z + nz - jump) % nz, (z + jump) % nz)
     my_rows = pl.ds(pl.multiple_of(y * HD, HD), HD)
+    share = hz // nx * HD
+    my_cols = pl.ds(pl.multiple_of(x * share, HD), share)
 
     counter = {"send": 0, "recv": 0, "local": 0}
 
@@ -169,6 +185,8 @@
     weight_in.start()
 
     partners = [dev_sib, dev_up, dev_down]
+    partners += [dev(up, y, x, sib), dev(down, y, x, sib)]
+    partners += [dev(z_jump[0], y, x, c), dev(z_jump[1], y, x, c)]
     for dy in range(1, NY):
         for cc in range(2):
             partners.append(dev(z, (y + dy) % NY, x, cc))
@@ -190,13 +208,6 @@
             mine, dst = src.at[:, j * HD : (j + 1) * HD], buf[name].at[z, part, :]
             send(mine, dst, base, dev(z, y_to, x, half_y), own)
             keep(mine, dst, base, own)
-    for j in range(2):
-        y_to = 2 * c + j
-        for cc in range(2):
-            own = jnp.logical_and(y_to == y, c == cc)
-            mine, dst = q_ref.at[:, j * HD : (j + 1) * HD], buf["qh"].at[my_rows, :]
-            send(mine, dst, id_q, dev(z, y_to, x, cc), own)
-            keep(mine, dst, id_q, own)
     id_w = alloc("recv")
     send(w_ref.at[:, pl.ds(other_half, dh)], buf["weight"].at[c], id_w, dev_sib, single=True)
 
@@ -248,6 +259,13 @@
             for h in range(2):
                 dst, recv_id = row_slot(g), id_step_one + 2 * side + c
                 send(buf["picked"].at[h], dst, recv_id, dev(z, y, to, h), single=True)
+    for j in range(2):
+        y_to = 2 * c + j
+        for cc in range(2):
+            own = jnp.logical_and(y_to == y, c == cc)
+            mine, dst = q_ref.at[:, j * HD : (j + 1) * HD], buf["qh"].at[my_rows, :]
+            send(mine, dst, id_q, dev(z, y_to, x, cc), own)
+            keep(mine, dst, id_q, own)
     rows[pl.ds(pl.multiple_of(g * cap, cap), cap), :] = buf["picked"][c]
 
     buf["dkp"][...] = jnp.zeros_like(buf["dkp"])
@@ -258,24 +276,41 @@
     soft[HD : HD + 8, :] = jnp.full((8, NY * HD), NEG, F32)
 
     halves = (slice(0, HD), slice(HD, 2 * HD))
-    ring = [
-        (name, half, n_up, n_down)
-        for name, n_up, n_down in (("kk", lay.far, lay.near), ("vv", lay.near, lay.far))
-        for half in range(2)
-    ]
+    ring = [(name, half, FAR_WAY[name]) for name in ("kk", "vv") for half in range(2)]
+    dev_next = (dev_down, dev_up)
+
+    needed = lay.needed
+
+    def source(direction, d):
+        return (z + d) % nz if direction == 0 else (z + nz - d) % nz
 
     def ring_step(t):
-        for name, half, n_up, n_down in ring:
+        for name, half, far_way in ring:
             if t == 0 and half == 0:
                 recv(buf[name].at[z], id_k if name == "kk" else id_v)
-            for side, hops in ((0, n_up), (1, n_down)):
-                b = (z + nz - t) % nz if side == 0 else (z + t) % nz
+            for direction in (1, 0):
+                b = source(direction, t)
                 ref = buf[name].at[b, halves[half], :]
-                if 1 <= t <= hops:
-                    recv(ref, ident(name, half, t, side))
-                if t + 1 <= hops:
-                    to = dev_up if side == 0 else dev_down
-                    send(ref, ref, ident(name, half, t + 1, side), to)
+                is_far = direction == far_way
+
+                def useless(d):
+                    return jnp.logical_not(needed(b, direction == 0, d, is_far))
+
+                if 1 <= t <= near:
+                    recv(ref, ident(name, half, direction, t), useless(t))
+                if t + 1 <= near:
+                    key = ident(name, half, direction, t + 1)
+                    send(ref, ref, key, dev_next[direction], useless(t + 1))
+                if t == relay and is_far:
+                    to = dev(z_jump[direction], y, x, c)
+                    send(ref, ref, ident(name, half, direction, far), to, useless(far))
+
+    def ring_far():
+        for name, half, far_way in ring:
+            b = source(far_way, far)
+            ref = buf[name].at[b, halves[half], :]
+            useless = jnp.logical_not(needed(b, far_way == 0, far, True))
+            recv(ref, ident(name, half, far_way, far), useless)
 
     ring_step(0)
 
@@ -363,27 +398,31 @@
 
         for dy in range(1, NY):
             y_to = (y + dy) % NY
-            send(
-                buf["slice_out"].at[y_to],
-                buf["slices"].at[my_rows, :],
-                id_slice,
-                dev(z, y_to, x, c),
-                single=True,
-            )
-        buf["slices"][my_rows, :] = buf["slice_out"][y]
+            src, dst = buf["slice_out"].at[y_to, :, my_cols], buf["slices"].at[my_rows, my_cols]
+            send(src, dst, id_slice, dev(z, y_to, x, c), single=True)
+        buf["slices"][my_rows, my_cols] = buf["slice_out"][y, :, my_cols]
 
     rows_step_two()
-    recv(buf["qh"], id_q)
-    forward_block(z, True)
-    for t in range(1, lay.far + 1):
-        ring_step(t)
-        if t == min(2, lay.far):
+    for t in range(1, far + 1):
+        if t <= near:
+            ring_step(t)
+        else:
+            ring_far()
+        if t == 1:
+            recv(buf["qh"], id_q)
+            forward_block(z, True)
+        if t == min(2, far):
             project()
             out_gradient()
         forward_pair(t)
 
     id_soft = alloc("recv")
     send(soft, buf["soft_in"], id_soft, dev_sib)
+    recv(buf["slices"].at[: (NY - 1) * HD, :share], id_slice)
+    id_slice_x = alloc("recv")
+    for dx in range(1, nx):
+        ref = buf["slices"].at[:, my_cols]
+        send(ref, ref, id_slice_x, dev(z, y, (x + dx) % nx, c), single=True)
     recv(buf["goh"], id_go)
     recv(buf["gates"].at[pl.ds(0, NY - 1)], id_gate)
     recv(buf["soft_in"], id_soft)
@@ -438,71 +477,102 @@
         if t <= nz - 1 - t:
             pl.when(z + t >= nz)(lambda: backward_block((z + t) % nz, False))
 
-    hops = ((lay.far, lay.near), (lay.near, lay.far))
-
     def target(direction, d):
         return (z + nz - d) % nz if direction == 0 else (z + d) % nz
 
-    dev_next = (dev_down, dev_up)
+    id_kv_fin, id_dq = alloc("recv"), alloc("recv")
+    side = y % 2
+
+    def kv_part(kind, b, part):
+        return (buf["dkp"] if kind == 0 else buf["dvp"]).at[b, part, :]
+
+    def kv_useless(b, kind, direction, d):
+        return jnp.logical_not(needed(b, direction == 1, d, direction == kind))
+
+    def kv_far():
+        for kind in range(2):
+            b = target(kind, far)
+            useless = kv_useless(b, kind, kind, far)
+            for part in halves:
+                out = buf["kv_send"].at[kind, kind, near, part, :]
+                out[...] = kv_part(kind, b, part)[...].astype(BF)
+                key = ident("chain", kind, kind, part.start, near)
+                to = dev(z_jump[kind], y, x, c)
+                send(out, buf["kv_recv"].at[kind, kind, near, part, :], key, to, useless)
+
+    def kv_taken(total, kind, direction, t, part, useless):
+        ref = buf["kv_recv"].at[kind, direction, t, part, :]
+        recv(ref, ident("chain", kind, direction, part.start, t), useless)
+
+        @pl.when(jnp.logical_not(useless))
+        def _():
+            total[...] += ref[...].astype(F32)
 
     def kv_step(t):
-        inc = buf["kv_recv"]
+        d = near - t
         for kind in range(2):
             for part in halves:
                 for direction in range(2):
-                    n = hops[kind][direction]
-                    if t >= n:
-                        continue
-                    key = ("chain", kind, direction, part.start)
-                    b = target(direction, n - t)
-                    total = (buf["dkp"] if kind == 0 else buf["dvp"])[b, part, :]
+                    b = target(direction, d)
+                    total = kv_part(kind, b, part)
                     if t > 0:
-                        recv(inc.at[kind, direction, t - 1, part, :], ident(*key, t - 1))
-                        total = total + inc[kind, direction, t - 1, part, :].astype(F32)
+                        useless = kv_useless(b, kind, direction, d + 1)
+                        kv_taken(total, kind, direction, t - 1, part, useless)
+                    if d == relay and direction == kind:
+                        useless = kv_useless(b, kind, direction, far)
+                        kv_taken(total, kind, direction, near, part, useless)
                     out = buf["kv_send"].at[kind, direction, t, part, :]
-                    out[...] = total.astype(BF)
-                    to = dev_next[direction]
-                    send(out, inc.at[kind, direction, t, part, :], ident(*key, t), to)
-
-    def kv_last(kind, part):
-        inc = buf["kv_recv"]
-        total = (buf["dkp"] if kind == 0 else buf["dvp"])[z, part, :]
-        for direction in range(2):
-            n = hops[kind][direction]
-            if n > 0:
-                last = ident("chain", kind, direction, part.start, n - 1)
-                recv(inc.at[kind, direction, n - 1, part, :], last)
-                total = total + inc[kind, direction, n - 1, part, :].astype(F32)
-        return total
+                    useless = kv_useless(b, kind, direction, d)
+
+                    @pl.when(jnp.logical_not(useless))
+                    def _():
+                        out[...] = total[...].astype(BF)
+
+                    if d > 1:
+                        key = ident("chain", kind, direction, part.start, t)
+                        dst = buf["kv_recv"].at[kind, direction, t, part, :]
+                        send(out, dst, key, dev_next[direction], useless)
+                    else:
+                        to = dev(down if direction == 0 else up, 2 * c + part.start // HD, x, half_y)
+                        dst = kv_land.at[direction, kind, side]
+                        send(out, dst, ident("land", direction, kind), to, useless)
 
     def dw_part(b, half):
         rows_of = buf["slices"][:, pl.ds(pl.multiple_of((b % hz) * HD, HD), HD)]
         return dot(rows_of, buf["outs"][:, half * 2 * HD : (half + 1) * 2 * HD], 0, 0)
 
+    def dw_send(half, direction, d, t, takes, to):
+        b = target(direction, d)
+        skip = b // hz != c
+        out, inc = buf["dw_send"].at[half, direction, t], buf["dw_recv"]
+        for u in takes:
+            recv(inc.at[half, direction, u], ident("dw", half, direction, u), skip)
+
+        @pl.when(jnp.logical_not(skip))
+        def _():
+            total = dw_part(b, half)
+            for u in takes:
+                total = total + inc[half, direction, u].astype(F32)
+            out[...] = total.astype(BF)
+
+        send(out, inc.at[half, direction, t], ident("dw", half, direction, t), to, skip)
+
+    def dw_far():
+        for half in range(2):
+            to = dev(z_jump[half], y, x, half if relay == 0 else c)
+            dw_send(half, half, far, near, [], to)
+
     def dw_step(t):
-        inc = buf["dw_recv"]
         for half in range(2):
             for direction in range(2):
-                n = hops[half][direction]
-                if t >= n:
-                    continue
-                b = target(direction, n - t)
-                skip = b // hz != c
-                out = buf["dw_send"].at[half, direction, t]
-                if t > 0:
-                    recv(inc.at[half, direction, t - 1], ident("dw", half, direction, t - 1), skip)
-
-                @pl.when(jnp.logical_not(skip))
-                def _():
-                    total = dw_part(b, half)
-                    if t > 0:
-                        total = total + inc[half, direction, t - 1].astype(F32)
-                    out[...] = total.astype(BF)
-
+                d = near - t
+                takes = [t - 1] if t > 0 else []
+                if d == relay and direction == half:
+                    takes.append(near)
                 to = dev_next[direction]
-                if t == n - 1:
+                if d == 1:
                     to = dev(down if direction == 0 else up, y, x, half)
-                send(out, inc.at[half, direction, t], ident("dw", half, direction, t), to, skip)
+                dw_send(half, direction, d, t, takes, to)
 
     id_dw_own = alloc("recv")
     not_holder = z // hz != c
@@ -524,14 +594,13 @@
             @pl.when(c == half)
             def _():
                 total = buf["dw_own"][...]
-                for direction in range(2):
-                    n = hops[half][direction]
-                    if n > 0:
-                        recv(
-                            buf["dw_recv"].at[half, direction, n - 1],
-                            ident("dw", half, direction, n - 1),
-                        )
-                        total = total + buf["dw_recv"][half, direction, n - 1].astype(F32)
+                takes = [(direction, near - 1) for direction in range(2) if near > 0]
+                if relay == 0:
+                    takes.append((half, near))
+                for direction, t in takes:
+                    ref = buf["dw_recv"].at[half, direction, t]
+                    recv(ref, ident("dw", half, direction, t))
+                    total = total + ref[...].astype(F32)
                 buf["dw_fin"][...] = total
 
     def share_outs():
@@ -541,7 +610,8 @@
             send(ref, ref, id_outs_sib, dev_sib)
 
     def take_outs():
-        recv(buf["slices"].at[: (NY - 1) * HD, :], id_slice)
+        if nx > 1:
+            recv(buf["slices"].at[:, : (nx - 1) * share], id_slice_x)
         recv(buf["outs"].at[: 2 * HD, : (NY - 1) * HD], id_outs_sib)
 
     id_router_x = alloc("recv")
@@ -571,19 +641,14 @@
         sig = 1.0 / (1.0 + jnp.exp(-logit_row))
         lg_ref[...] = placed[0:1, :] * sig * (1.0 - sig)
 
-    id_kv_fin, id_dq = alloc("recv"), alloc("recv")
-    side = y % 2
-
-    def send_key_value_grads():
+
+    def send_own_part():
         for kind in range(2):
             for j in range(2):
-                final = kv_last(kind, halves[j])
-                if kind == 0:
-                    final = final * factor
-                buf["kv_fin"][kind, j] = final.astype(BF)
+                buf["kv_fin"][kind, j] = kv_part(kind, z, halves[j])[...].astype(BF)
                 y_to = 2 * c + j
                 own = jnp.logical_and(y_to == y, half_y == c)
-                src, dst = buf["kv_fin"].at[kind, j], kv_land.at[kind, side]
+                src, dst = buf["kv_fin"].at[kind, j], kv_land.at[2, kind, side]
                 send(src, dst, id_kv_fin, dev(z, y_to, x, half_y), own)
                 keep(src, dst, id_kv_fin, own)
 
@@ -595,33 +660,40 @@
             send(src, dst, id_dq, dev(z, i, x, half_y), own)
             keep(src, dst, id_dq, own)
 
-    for d in range(lay.far, 0, -1):
+    for d in range(far, 0, -1):
         backward_pair(d)
-        if d == max(lay.near, 1):
+        if d == far:
+            kv_far()
+        if d == near:
             kv_step(0)
     backward_block(z, True)
     send_query_grads()
-    if lay.far > 1:
+    send_own_part()
+    share_outs()
+    if near > 1:
         kv_step(1)
-    share_outs()
     router_send()
     take_outs()
-    dw_step(0)
-    for t in range(2, lay.far):
+    dw_far()
+    if near > 0:
+        dw_step(0)
+    for t in range(2, near):
         kv_step(t)
         dw_step(t - 1)
-    send_key_value_grads()
     dw_own_block()
     router_last()
-    if lay.far > 1:
-        dw_step(lay.far - 1)
-
+    if near > 1:
+        dw_step(near - 1)
     dw_last()
     dw_out = pltpu.make_async_copy(buf["dw_fin"], dw_land, local_sems.at[alloc("local")])
     dw_out.start()
 
     recv(dq_land, id_dq)
-    recv(kv_land, id_kv_fin)
+    recv(kv_land.at[2], id_kv_fin)
+    for direction in range(2):
+        for kind in range(2):
+            useless = kv_useless(z, kind, direction, 1)
+            recv(kv_land.at[direction, kind], ident("land", direction, kind), useless)
     dw_out.wait()
     for entry in pool + singles:
         if entry is not None:
@@ -629,17 +701,23 @@
 
 
 POOL = 24
-RECV_SEMS = 92
-SEND_SEMS = 35
+RECV_SEMS = 89
+SEND_SEMS = 38
 VMEM_LIMIT = 60 * 1024 * 1024
 
 
-def finish(dq_land, kv_land, dw_land, lg_in, dq_ref, dk_ref, dv_ref, dw_ref, lg_ref):
+def finish(nz, dq_land, kv_land, dw_land, lg_in, dq_ref, dk_ref, dv_ref, dw_ref, lg_ref):
+    lay = Layout(nz, 1, HD, HD, HD)
+    z = lax.axis_index("seq") // NY
     for j in range(2):
         cols = slice(j * HD, (j + 1) * HD)
         dq_ref[:, cols] = (dq_land[j, 0].astype(F32) + dq_land[j, 1].astype(F32)).astype(BF)
-        dk_ref[:, cols] = kv_land[0, j]
-        dv_ref[:, cols] = kv_land[1, j]
+        for kind, ref, scale in ((0, dk_ref, HD ** (-0.5)), (1, dv_ref, 1.0)):
+            total = kv_land[2, kind, j].astype(F32)
+            for way in range(2):
+                useful = lay.needed(z, way == 1, 1, way == kind)
+                total = total + jnp.where(useful, kv_land[way, kind, j].astype(F32), 0.0)
+            ref[:, cols] = (total * scale).astype(BF)
     dw_ref[...] = dw_land[...]
     lg_ref[...] = lg_in[...]
 
@@ -660,7 +738,7 @@
             kernel,
             out_shape=(
                 jax.ShapeDtypeStruct((2, 2, HD, HD), BF),
-                jax.ShapeDtypeStruct((2, 2, HD, HD), BF),
+                jax.ShapeDtypeStruct((3, 2, 2, HD, HD), BF),
                 jax.ShapeDtypeStruct((HD, 2 * HD), F32),
                 jax.ShapeDtypeStruct((1, HD), F32),
             ),
@@ -678,7 +756,7 @@
             name="routed_backward",
         )(grad, logit.reshape(1, -1), index, count, weight, q, k, v)
         out = pl.pallas_call(
-            finish,
+            functools.partial(finish, nz),
             out_shape=(
                 jax.ShapeDtypeStruct(q.shape, BF),
                 jax.ShapeDtypeStruct(q.shape, BF),

time: 60.1 us -> 57.6 us (0.958)
  Pallas kernels: 59.4 us -> 56.8 us
    pallas_call x1, Pallas kernels: 57.6 us -> 55 us  [run(): pl.pallas_call(kernel, out_shape=(jax.ShapeDtypeStruct((2, 2, HD, HD), BF...]
where the time goes in v6:
time: 57.6 us; the launch traced here: 57.5 us
  Pallas kernels  56.8 us (99%)
  between operations  0.64 us (1%)
    pallas_call x1, Pallas kernels, run(): pl.pallas_call(kernel, out_shape=(jax.ShapeDtypeStruct((2, 2, HD, HD), BF...  55 us
    pallas_call x1, Pallas kernels, run(): pl.pallas_call(functools.partial(finish, nz), out_shape=(jax.ShapeDtypeSt...  1.84 us

profile of v6, /device:TPU:1, one launch (start us, length us, event | category | flops | bytes accessed | tf_op | source)
XLA Modules:
  0.0 57.5 jit_solution(6371895306004954556)
XLA Ops:
  0.6 55.0 %routed_backward.1 = (bf16[2,2,128,128]{3,2,1,0:T(8,128)(2,1)}, bf16[3,2,2,128,128]{4,3,2,1,0:T(8,128)(2,1)}, f32[128,256]{1,0:T(8,128)}, f32[1,128]{1,0:T(1,128)}) custom-call(bf16[128,4096]{1,0:T(8,128)(2,1)} %refs_0_.1, f32[1,128]{1,0:T(1,128)} %bitcast.2, s32[32]{0:T(128)} %refs_2_.1, s32[256]{0:T(256)} %refs_3_.1, bf16[256,4096]{1,0:T(8,128)(2,1)} %refs_4_.1, ...), custom_call_target="tpu_custom_call" | custom-call | tf_op jit(solution)/shard_map/routed_backward/pallas_call | solution.py:737
  55.6 1.8 %finish.1 = (bf16[128,256]{1,0:T(8,128)(2,1)}, bf16[128,256]{1,0:T(8,128)(2,1)}, bf16[128,256]{1,0:T(8,128)(2,1)}, f32[128,256]{1,0:T(8,128)}, f32[1,128]{1,0:T(1,128)}) custom-call(bf16[2,2,128,128]{3,2,1,0:T(8,128)(2,1)} %get-tuple-element.14.dq_land, bf16[3,2,2,128,128]{4,3,2,1,0:T(8,128)(2,1)} %get-tuple-element.15.kv_land, ...), custom_call_target="tpu_custom_call" | custom-call | tf_op jit(solution)/shard_map/finish/pallas_call | solution.py:758

commit v7 on v6

--- a/solution.py
+++ b/solution.py
@@ -62,6 +62,8 @@
             soft=v((HD + 16, NY * HD), F32),
             soft_in=v((HD + 16, NY * HD), F32),
             lse=v((8, NY * HD), F32),
+            scales=v((16, NY * HD), F32),
+            outs_t=v((HD, NY * HD), F32),
             delta=v((8, NY * HD), F32),
             outs=v((NY * HD, NY * HD), BF),
             dqt=v((HD, NY * HD), F32),
@@ -69,6 +71,7 @@
             dvp=v((nz, 2 * HD, HD), F32),
             dw_mine=v((2, HD, 2 * HD), F32),
             dw_own=v((HD, 2 * HD), F32),
+            dw_acc=v((2, 2, HD, 2 * HD), F32),
             kv_send=v((2, 2, steps, 2 * HD, HD), BF),
             kv_recv=v((2, 2, steps, 2 * HD, HD), BF),
             dw_send=v((2, 2, steps, HD, 2 * HD), BF),
@@ -186,7 +189,7 @@
 
     partners = [dev_sib, dev_up, dev_down]
     partners += [dev(up, y, x, sib), dev(down, y, x, sib)]
-    partners += [dev(z_jump[0], y, x, c), dev(z_jump[1], y, x, c)]
+    partners += [dev(zz, y, x, cc) for zz in z_jump for cc in range(2)]
     for dy in range(1, NY):
         for cc in range(2):
             partners.append(dev(z, (y + dy) % NY, x, cc))
@@ -423,7 +426,6 @@
     for dx in range(1, nx):
         ref = buf["slices"].at[:, my_cols]
         send(ref, ref, id_slice_x, dev(z, y, (x + dx) % nx, c), single=True)
-    recv(buf["goh"], id_go)
     recv(buf["gates"].at[pl.ds(0, NY - 1)], id_gate)
     recv(buf["soft_in"], id_soft)
     head_cols = pl.ds(pl.multiple_of(y * HD, HD), HD)
@@ -433,17 +435,8 @@
     scale_a, scale_b = jnp.exp2(max_a - top), jnp.exp2(max_b - top)
     norm = soft[HD + 8 : HD + 9, :] * scale_a + soft_in[HD + 8 : HD + 9, :] * scale_b
     buf["lse"][0:1, :] = top + jnp.log2(norm)
-    scale_a, scale_b = scale_a / norm, scale_b / norm
-    for i in range(NY):
-        span = slice(i * HD, (i + 1) * HD)
-        out_t = soft[0:HD, span] * scale_a[:, span] + soft_in[0:HD, span] * scale_b[:, span]
-        out_t = out_t.astype(BF).astype(F32)
-        gate_row = buf["gates"][i, 0:1, :]
-        buf["outs"][span, head_cols] = (gate_row * out_t).T.astype(BF)
-        delta = jnp.sum(out_t * buf["goh"][span, :].astype(F32).T, axis=0, keepdims=True)
-        buf["delta"][0:1, span] = delta
-        buf["router_out"][i] = jnp.broadcast_to(delta / gate_row, (8, HD))
-
+    buf["scales"][0:1, :] = scale_a / norm
+    buf["scales"][8:9, :] = scale_b / norm
     id_outs, id_outs_sib, id_router_y = alloc("recv"), alloc("recv"), alloc("recv")
 
     def out_part(head, core):
@@ -452,10 +445,30 @@
             pl.ds(pl.multiple_of(head * HD, HD), HD),
         ]
 
+    for i in range(NY):
+        piece = (2 * c + i) % NY
+        span = pl.ds(pl.multiple_of(piece * HD, HD), HD)
+        out_t = soft[0:HD, span] * buf["scales"][0:1, span] + soft_in[0:HD, span] * buf["scales"][8:9, span]
+        out_t = out_t.astype(BF).astype(F32)
+        buf["outs_t"][:, span] = out_t
+        gate_row = buf["gates"][piece, 0:1, :]
+        buf["outs"][span, head_cols] = (gate_row * out_t).T.astype(BF)
+        if i == 1:
+            for dy in range(1, NY):
+                to = dev(z, (y + dy) % NY, x, c)
+                send(out_part(y, c), out_part(y, c), id_outs, to)
+    recv(buf["goh"], id_go)
+    for i in range(NY):
+        span = slice(i * HD, (i + 1) * HD)
+        out_t = buf["outs_t"][:, span]
+        gate_row = buf["gates"][i, 0:1, :]
+        delta = jnp.sum(out_t * buf["goh"][span, :].astype(F32).T, axis=0, keepdims=True)
+        buf["delta"][0:1, span] = delta
+        buf["router_out"][i] = jnp.broadcast_to(delta / gate_row, (8, HD))
+
     for dy in range(1, NY):
         y_to = (y + dy) % NY
         to = dev(z, y_to, x, c)
-        send(out_part(y, c), out_part(y, c), id_outs, to)
         send(buf["router_out"].at[y_to], buf["router_y"].at[y], id_router_y, to)
     buf["router_y"][y] = buf["router_out"][y]
 
@@ -541,38 +554,42 @@
         rows_of = buf["slices"][:, pl.ds(pl.multiple_of((b % hz) * HD, HD), HD)]
         return dot(rows_of, buf["outs"][:, half * 2 * HD : (half + 1) * 2 * HD], 0, 0)
 
-    def dw_send(half, direction, d, t, takes, to):
-        b = target(direction, d)
-        skip = b // hz != c
-        out, inc = buf["dw_send"].at[half, direction, t], buf["dw_recv"]
-        for u in takes:
-            recv(inc.at[half, direction, u], ident("dw", half, direction, u), skip)
-
-        @pl.when(jnp.logical_not(skip))
-        def _():
-            total = dw_part(b, half)
-            for u in takes:
-                total = total + inc[half, direction, u].astype(F32)
-            out[...] = total.astype(BF)
-
-        send(out, inc.at[half, direction, t], ident("dw", half, direction, t), to, skip)
-
-    def dw_far():
-        for half in range(2):
-            to = dev(z_jump[half], y, x, half if relay == 0 else c)
-            dw_send(half, half, far, near, [], to)
-
-    def dw_step(t):
+    def dw_ways(d):
         for half in range(2):
             for direction in range(2):
-                d = near - t
-                takes = [t - 1] if t > 0 else []
-                if d == relay and direction == half:
-                    takes.append(near)
+                if d < far or direction == half:
+                    b = target(direction, d)
+                    yield half, direction, b, b // hz != c
+
+    def dw_ready():
+        for half, direction, b, skip in dw_ways(2):
+
+            @pl.when(jnp.logical_not(skip))
+            def _():
+                buf["dw_acc"][half, direction] = dw_part(b, half)
+
+    def dw_send(d):
+        inc = buf["dw_recv"]
+        for half, direction, b, skip in dw_ways(d):
+            out = buf["dw_send"].at[half, direction, d - 1]
+            takes = [u for u in (3, 4) if d == 2 and (u < far or direction == half)]
+            for u in takes:
+                recv(inc.at[half, direction, u - 1], ident("dw", half, direction, u), skip)
+
+            @pl.when(jnp.logical_not(skip))
+            def _():
+                total = buf["dw_acc"][half, direction] if d == 2 else dw_part(b, half)
+                for u in takes:
+                    total = total + inc[half, direction, u - 1].astype(F32)
+                out[...] = total.astype(BF)
+
+            if d == far:
+                to = dev(z_jump[direction], y, x, c)
+            elif d == 3:
                 to = dev_next[direction]
-                if d == 1:
-                    to = dev(down if direction == 0 else up, y, x, half)
-                dw_send(half, direction, d, t, takes, to)
+            else:
+                to = dev(b, y, x, half)
+            send(out, inc.at[half, direction, d - 1], ident("dw", half, direction, d), to, skip)
 
     id_dw_own = alloc("recv")
     not_holder = z // hz != c
@@ -594,13 +611,11 @@
             @pl.when(c == half)
             def _():
                 total = buf["dw_own"][...]
-                takes = [(direction, near - 1) for direction in range(2) if near > 0]
-                if relay == 0:
-                    takes.append((half, near))
-                for direction, t in takes:
-                    ref = buf["dw_recv"].at[half, direction, t]
-                    recv(ref, ident("dw", half, direction, t))
-                    total = total + ref[...].astype(F32)
+                for d in (1, 2):
+                    for direction in range(2):
+                        ref = buf["dw_recv"].at[half, direction, d - 1]
+                        recv(ref, ident("dw", half, direction, d))
+                        total = total + ref[...].astype(F32)
                 buf["dw_fin"][...] = total
 
     def share_outs():
@@ -674,16 +689,14 @@
         kv_step(1)
     router_send()
     take_outs()
-    dw_far()
-    if near > 0:
-        dw_step(0)
-    for t in range(2, near):
-        kv_step(t)
-        dw_step(t - 1)
+    dw_send(4)
+    dw_send(3)
+    dw_send(1)
+    dw_ready()
+    kv_step(2)
     dw_own_block()
     router_last()
-    if near > 1:
-        dw_step(near - 1)
+    dw_send(2)
     dw_last()
     dw_out = pltpu.make_async_copy(buf["dw_fin"], dw_land, local_sems.at[alloc("local")])
     dw_out.start()

time: 57.6 us -> 56.6 us (0.983)
  Pallas kernels: 56.8 us -> 55.8 us
    pallas_call x1, Pallas kernels: 55 us -> 54 us  [run(): pl.pallas_call(kernel, out_shape=(jax.ShapeDtypeStruct((2, 2, HD, HD), BF...]
where the time goes in v7:
time: 56.6 us; the launch traced here: 56.5 us
  Pallas kernels  55.8 us (99%)
  between operations  0.64 us (1%)
    pallas_call x1, Pallas kernels, run(): pl.pallas_call(kernel, out_shape=(jax.ShapeDtypeStruct((2, 2, HD, HD), BF...  54 us
    pallas_call x1, Pallas kernels, run(): pl.pallas_call(functools.partial(finish, nz), out_shape=(jax.ShapeDtypeSt...  1.84 us

profile of v7, /device:TPU:1, one launch (start us, length us, event | category | flops | bytes accessed | tf_op | source)
XLA Modules:
  0.0 56.5 jit_solution(11239542282050998074)
XLA Ops:
  0.6 54.0 %routed_backward.1 = (bf16[2,2,128,128]{3,2,1,0:T(8,128)(2,1)}, bf16[3,2,2,128,128]{4,3,2,1,0:T(8,128)(2,1)}, f32[128,256]{1,0:T(8,128)}, f32[1,128]{1,0:T(1,128)}) custom-call(bf16[128,4096]{1,0:T(8,128)(2,1)} %refs_0_.1, f32[1,128]{1,0:T(1,128)} %bitcast.2, s32[32]{0:T(128)} %refs_2_.1, s32[256]{0:T(256)} %refs_3_.1, bf16[256,4096]{1,0:T(8,128)(2,1)} %refs_4_.1, ...), custom_call_target="tpu_custom_call" | custom-call | tf_op jit(solution)/shard_map/routed_backward/pallas_call | solution.py:750
  54.6 1.8 %finish.1 = (bf16[128,256]{1,0:T(8,128)(2,1)}, bf16[128,256]{1,0:T(8,128)(2,1)}, bf16[128,256]{1,0:T(8,128)(2,1)}, f32[128,256]{1,0:T(8,128)}, f32[1,128]{1,0:T(1,128)}) custom-call(bf16[2,2,128,128]{3,2,1,0:T(8,128)(2,1)} %get-tuple-element.14.dq_land, bf16[3,2,2,128,128]{4,3,2,1,0:T(8,128)(2,1)} %get-tuple-element.15.kv_land, ...), custom_call_target="tpu_custom_call" | custom-call | tf_op jit(solution)/shard_map/finish/pallas_call | solution.py:771

commit v8 on v7

--- a/solution.py
+++ b/solution.py
@@ -687,11 +687,11 @@
     share_outs()
     if near > 1:
         kv_step(1)
-    router_send()
     take_outs()
     dw_send(4)
     dw_send(3)
     dw_send(1)
+    router_send()
     dw_ready()
     kv_step(2)
     dw_own_block()

time: 56.6 us -> 56.9 us (level)
  no operation moved by 1% of the time
where the time goes in v8:
time: 56.9 us; the launch traced here: 56.7 us
  Pallas kernels  56.1 us (99%)
  between operations  0.64 us (1%)
    pallas_call x1, Pallas kernels, run(): pl.pallas_call(kernel, out_shape=(jax.ShapeDtypeStruct((2, 2, HD, HD), BF...  54.3 us
    pallas_call x1, Pallas kernels, run(): pl.pallas_call(functools.partial(finish, nz), out_shape=(jax.ShapeDtypeSt...  1.84 us

profile of v8, /device:TPU:1, one launch (start us, length us, event | category | flops | bytes accessed | tf_op | source)
XLA Modules:
  0.0 56.7 jit_solution(12304894312458007724)
XLA Ops:
  0.6 54.3 %routed_backward.1 = (bf16[2,2,128,128]{3,2,1,0:T(8,128)(2,1)}, bf16[3,2,2,128,128]{4,3,2,1,0:T(8,128)(2,1)}, f32[128,256]{1,0:T(8,128)}, f32[1,128]{1,0:T(1,128)}) custom-call(bf16[128,4096]{1,0:T(8,128)(2,1)} %refs_0_.1, f32[1,128]{1,0:T(1,128)} %bitcast.2, s32[32]{0:T(128)} %refs_2_.1, s32[256]{0:T(256)} %refs_3_.1, bf16[256,4096]{1,0:T(8,128)(2,1)} %refs_4_.1, ...), custom_call_target="tpu_custom_call" | custom-call | tf_op jit(solution)/shard_map/routed_backward/pallas_call | solution.py:750
  54.9 1.8 %finish.1 = (bf16[128,256]{1,0:T(8,128)(2,1)}, bf16[128,256]{1,0:T(8,128)(2,1)}, bf16[128,256]{1,0:T(8,128)(2,1)}, f32[128,256]{1,0:T(8,128)}, f32[1,128]{1,0:T(1,128)}) custom-call(bf16[2,2,128,128]{3,2,1,0:T(8,128)(2,1)} %get-tuple-element.14.dq_land, bf16[3,2,2,128,128]{4,3,2,1,0:T(8,128)(2,1)} %get-tuple-element.15.kv_land, ...), custom_call_target="tpu_custom_call" | custom-call | tf_op jit(solution)/shard_map/finish/pallas_call | solution.py:771
